TPU v7x, 32 devices: a whole 2x2x4 slice. The times are simulated.
32 devices in a mesh: groups: 2 (over x), tm: 16 (over z, y, core).
Axes of the slice: x: 2, y: 2, z: 4, core: 2. Of those that a mesh axis runs over, the one named last changes fastest.
Arguments:
- signal: bfloat16 [128, 4096], P('groups', 'tm'), parts along dimension 0, may hold values from -6 to 6
- codes: bfloat16 [128, 128, 4096], P('groups', None, 'tm'), parts along dimension 0, may hold values from -6 to 6
- filters: float32 [128, 256], replicated, may hold values from -0.03125 to 0.03125
Outputs:
- new_codes: bfloat16 [128, 128, 4096], P('groups', None, 'tm'), parts along dimension 0
- new_filters: float32 [256, 256], P('groups'), parts along dimension 0
There are 2 independent parts, one for each index of `groups`. A program takes and returns all parts, laid end to end along the dimension named above; an argument that names none is the same for every part. Nothing has to cross between parts.
All inputs are finite; a program needn't handle non-finite values.
Results may differ from a plain program's by a relative error of at most 0.0052.
Values may be sent and summed in bfloat16 or wider, within the bound.
No kernel may reach another device: no remote copies, remote signals or barrier semaphores. Data moves between devices by JAX's collectives and lax.ppermute only.
A program may use at most 192 MiB of HBM per device.

v0:
```python
import jax
import jax.numpy as jnp
from jax import lax
from jax.sharding import PartitionSpec as P

ETA_CODE = 2.0
LAM = 0.1
ETA_FILT = 0.5
EPS = 1e-06


def passed_along(block, axis, distance):
    devices = range(lax.axis_size(axis))
    route = [(i - distance, i) for i in devices if i - distance in devices]
    return lax.ppermute(block, axis, route)


def toeplitz(dict_b):
    count, taps = dict_b.shape
    padded = jnp.concatenate([dict_b, jnp.zeros((count, 1), dict_b.dtype)], axis=1)
    row_pos = lax.broadcasted_iota(jnp.int32, (taps, 2 * taps), 0)
    col_pos = lax.broadcasted_iota(jnp.int32, (taps, 2 * taps), 1)
    offset = col_pos - row_pos
    inside = jnp.logical_and(offset >= 0, offset < taps)
    lookup = jnp.where(inside, offset, taps)
    return jnp.take(padded, lookup, axis=1)


def hankel(extended, taps):
    row_pos = lax.broadcasted_iota(jnp.int32, (taps, taps), 0)
    col_pos = lax.broadcasted_iota(jnp.int32, (taps, taps), 1)
    return jnp.take(extended, row_pos + col_pos, axis=2)


def normalize(stepped):
    return stepped / jnp.sqrt(jnp.sum(stepped * stepped, axis=1, keepdims=True) + EPS)


def local_step(codes, signal, table, carry_in, error_in):
    chans, count, local_len = codes.shape
    taps = table.shape[1]
    blocks = local_len // taps
    blocked = codes.reshape(chans, count, blocks, taps)
    spread = jnp.einsum("cknb,kbs->cns", blocked, table, preferred_element_type=jnp.float32)
    lower = spread[:, :, :taps]
    upper = spread[:, :, taps:]
    carried = carry_in(codes, upper)
    before = jnp.concatenate([carried[:, None], upper[:, : blocks - 1]], axis=1)
    recon = (lower + before).reshape(chans, local_len)
    err = (recon - signal.astype(jnp.float32)).astype(jnp.bfloat16)
    err_blocks = err.reshape(chans, blocks, taps)
    following = error_in(err_blocks)
    after = jnp.concatenate([err_blocks[:, 1:], following[:, None]], axis=1)
    extended = jnp.concatenate([err_blocks, after], axis=2)
    grad_codes = jnp.einsum("cns,kts->cknt", extended, table, preferred_element_type=jnp.float32)
    moved = codes.astype(jnp.float32) - ETA_CODE * grad_codes.reshape(chans, count, local_len)
    new_codes = (moved - jnp.clip(moved, -LAM, LAM)).astype(jnp.bfloat16)
    windows = hankel(extended, taps)
    grad_terms = jnp.einsum("cknt,cnta->ka", blocked, windows, preferred_element_type=jnp.float32)
    return (new_codes, grad_terms)


def shards(signal, codes, filters):
    chans, count, local_len = codes.shape
    taps = filters.shape[1]
    devices = lax.axis_size("tm")
    dict_b = filters.astype(jnp.bfloat16)
    table = toeplitz(dict_b)
    scale_total = chans * local_len * devices

    def carry_codes(block_codes, upper):
        previous = passed_along(block_codes, "tm", 1)
        return jnp.einsum(
            "ckb,kbs->cs", previous, table[:, :, taps:], preferred_element_type=jnp.float32
        )

    def error_next(err_blocks):
        return passed_along(err_blocks[:, 0], "tm", -1)

    new_codes, grad_terms = local_step(codes, signal, table, carry_codes, error_next)
    summed = lax.psum(grad_terms, "tm")
    new_filters = normalize(filters - ETA_FILT * (summed / scale_total))
    return (new_codes, new_filters)


def solution(mesh):
    return jax.shard_map(
        shards,
        mesh=mesh,
        in_specs=(P("groups", "tm"), P("groups", None, "tm"), P()),
        out_specs=(P("groups", None, "tm"), P("groups", None)),
        check_vma=False,
    )
```

profile of v0, /device:TPU:0, one launch (start us, length us, event | category | flops | bytes accessed | tf_op | source)
XLA Modules:
  0.0 946.3 jit_solution(10255649181133351772)
XLA Ops:
  7.2 0.0 all-reduce.3.cloned.1.call-start
  7.2 6.5 copy.18
  13.7 4.3 collective-permute-start
  18.0 0.1 fusion.26
  18.1 0.1 fusion.33
  18.3 0.1 copy.16
  18.4 0.0 copy-start
  18.4 0.1 copy.28
  18.5 0.5 copy-done
  19.0 0.1 broadcast_clamp_fusion
  19.1 453.9 %gather_fusion = bf16[131072,128]{1,0:T(8,128)(2,1)} fusion(bf16[128,257]{0,1:T(8,128)(2,1)S(1)} %concatenate.6, s32[131072]{0:T(1024)S(1)} %broadcast_clamp_fusion), kind=kCustom, calls=%fused_computation | custom fusion | bytes 67633152 | tf_op jit(solution)/shard_map/jit(_take)/gather | solution.py:26
  473.0 44.0 %copy.17 = bf16[256,512,128]{1,2,0:T(8,128)(2,1)} copy(bf16[256,512,128]{2,1,0:T(8,128)(2,1)} %bitcast.67) | data formatting | bytes 67108864 | tf_op jit(solution)/shard_map/jit(_take)/gather | solution.py:26
  517.0 22.9 %select_bitcast_fusion = bf16[128,256,512]{2,0,1:T(8,128)(2,1)} fusion(bf16[256,512,128]{1,2,0:T(8,128)(2,1)} %copy.17, pred[256,512]{1,0:T(8,128)(4,1)S(1)} %fusion.33), kind=kLoop, calls=%fused_computation.2 | loop fusion | flops 16777216 | bytes 67239936 | tf_op jit(solution)/shard_map/jit(_take)/select_n | solution.py:26
  539.9 0.1 copy.29
  540.1 14.8 %convolution_bitcast_fusion = f32[64,1,512]{2,0,1:T(8,128)S(1)} fusion(bf16[64,128,256]{1,0,2:T(8,128)(2,1)} %copy.18, bf16[128,256,512]{2,0,1:T(8,128)(2,1)} %select_bitcast_fusion), kind=kOutput, calls=%fused_computation.16 | convolution fusion | flops 2147483648 | bytes 37879808 | tf_op jit(solution)/shard_map/cknb,kbs->cns/dot_general | solution.py:44
  554.9 10.1 %fusion.23 = bf16[64,256]{1,0:T(8,128)(2,1)S(1)} fusion(bf16[64,128,256]{1,0,2:T(8,128)(2,1)} %collective-permute-done, bf16[128,256,512]{2,0,1:T(8,128)(2,1)} %select_bitcast_fusion, f32[64,1,512]{2,0,1:T(8,128)S(1)} %convolution_bitcast_fusion, bf16[64,256]{1,0:T(8,128)(2,1)S(1)} %copy-done.3), kind=kOutput, calls=%fused_computation.21 | convolution fusion | flops 1073807360 | bytes 21102592 | tf_op jit(solution)/shard_map/ckb,kbs->cs/dot_general | solution.py:73
  565.0 1.5 collective-permute-start.1
  566.5 1.7 collective-permute-done.1
  568.2 18.0 %fusion.40 = f32[128,256,64]{0,2,1:T(8,128)} fusion(bf16[128,256,512]{2,0,1:T(8,128)(2,1)} %select_bitcast_fusion, bf16[64,1,256]{2,0,1:T(8,128)(2,1)S(1)} %bitcast.74, bf16[64,1,256]{2,0,1:T(8,128)(2,1)S(1)} %bitcast.72), kind=kOutput, calls=%fused_computation.45 | convolution fusion | flops 2147614720 | bytes 42008576 | tf_op jit(solution)/shard_map/cns,kts->cknt/dot_general | solution.py:55
  586.2 0.1 copy.21
  586.4 227.3 %gather_fusion.1 = bf16[65536,64]{1,0:T(8,128)(2,1)} fusion(bf16[64,512]{0,1:T(8,128)(2,1)S(1)} %copy.21, s32[65536]{0:T(1024)S(1)} %broadcast_clamp_fusion.1), kind=kCustom, calls=%fused_computation.1 | custom fusion | bytes 17039360 | tf_op jit(solution)/shard_map/jit(_take)/gather | solution.py:32
  813.7 25.1 %copy.22 = bf16[256,256,64]{0,1,2:T(8,128)(2,1)} copy(bf16[256,256,64]{2,1,0:T(8,128)(2,1)} %bitcast.68) | data formatting | bytes 16777216 | tf_op jit(solution)/shard_map/jit(_take)/gather | solution.py:32
  838.8 7.6 fusion.8
  846.3 0.0 all-reduce.3.cloned.1.call-update
  846.4 9.2 copy.27
  855.6 7.2 fusion.2
  862.8 0.0 copy-start.1
  862.8 4.4 copy.24
  867.3 69.5 %all-reduce.3.cloned.1.call-done = f32[128,256]{0,1:T(8,128)} async-done(((f32[128,256]{0,1:T(8,128)}), f32[128,256]{0,1:T(8,128)}) %all-reduce.3.cloned.1.call-update) | async-done | bytes 131088 | tf_op jit(solution)/shard_map/psum | solution.py:81
  936.8 1.0 multiply_reduce_fusion
  937.8 0.9 broadcast_divide_fusion
  938.7 0.8 copy.25
  (13 shorter events, 0.1 us)
Async XLA Ops:
  7.2 11.1 %copy-start.2 = (f32[128,256]{1,0:T(8,128)S(1)}, f32[128,256]{1,0:T(8,128)}, u32[]{:S(2)}) copy-start(f32[128,256]{1,0:T(8,128)} %param.5) | copy-start | bytes 393220
  7.2 929.6 %all-reduce.3.cloned.1.call-start = ((), (), s32[]{:S(2)}) async-start(), calls=%async_computation | async-start | bytes 262144 | tf_op jit(solution)/shard_map/psum | solution.py:81
  13.7 541.2 %collective-permute-start = (bf16[64,128,256]{1,0,2:T(8,128)(2,1)}, bf16[64,128,256]{1,0,2:T(8,128)(2,1)}, u32[]{:S(2)}, u32[]{:S(2)}) collective-permute-start(bf16[64,128,256]{1,0,2:T(8,128)(2,1)} %copy.18), channel_id=1, source_target_pairs={{0,1},{1,2},{2,3},{3,4},{4,5},{5,6},{6,7},{7,8},{8,9},{9,10},{10,1... | collective-permute-start | bytes 12582920 | tf_op jit(solution)/shard_map/ppermute | solution.py:15
  18.4 0.7 copy-start
  540.1 14.8 %copy-start.3 = (bf16[64,256]{1,0:T(8,128)(2,1)S(1)}, bf16[64,256]{1,0:T(8,128)(2,1)}, u32[]{:S(2)}) copy-start(bf16[64,256]{1,0:T(8,128)(2,1)} %param.3) | copy-start | bytes 98308
  565.0 3.3 collective-permute-start.1
  862.8 74.0 %copy-start.1 = (f32[128,256]{0,1:T(8,128)S(1)}, f32[128,256]{0,1:T(8,128)}, u32[]{:S(2)}) copy-start(f32[128,256]{0,1:T(8,128)} %copy-done) | copy-start | bytes 393220
Sparse Core Ops, SparseCore 0:
  846.5 90.2 all-reduce.2
where the time goes:
time: 949 us; the launch traced here: 946 us
  local copies, waits for them, and re-layouts  772 us (81%)
  waiting for transfers between devices  71.3 us (8%)
  matrix products  50.4 us (5%)
  other arithmetic  32.4 us (3%)
  between operations  14.2 us (1%)
    gather x2, local copies, waits for them, and re-layouts, toeplitz(): return jnp.take(padded, lookup, axis=1)  498 us
    gather x2, local copies, waits for them, and re-layouts, hankel(): return jnp.take(extended, row_pos + col_pos, axis=2)  252 us
    psum x1, waiting for transfers between devices, shards(): summed = lax.psum(grad_terms, 'tm')  69.5 us
    select_n x1, other arithmetic, toeplitz(): return jnp.take(padded, lookup, axis=1)  22.9 us
  transfers between devices with their start and end apart: 3, of which 2 were waited for; matrix products, arithmetic and copies ran while one was open for 59% of the time, Pallas kernels for 0%

commit v1 on v0

v1 whole, which is shorter than its diff:
```python
import functools

import jax
import jax.numpy as jnp
from jax import lax
from jax.experimental import pallas as pl
from jax.experimental.pallas import tpu as pltpu
from jax.sharding import PartitionSpec as P

ETA_CODE = 2.0
LAM = 0.1
ETA_FILT = 0.5
EPS = 1e-06

F32 = jnp.float32
BF16 = jnp.bfloat16
LANES = 128
GROUP = 8
CHUNKS = 4
PACK = 16
VMEM_BYTES = 16 << 20


def chunk_starts(chans):
    return [0, chans // 8, chans // 4, chans // 2, chans]


def fetch_parts(source, target, arrived, starts):
    copies = {}
    for step, first in enumerate(starts[:-1]):
        rows = pl.ds(first, starts[step + 1] - first)
        copies[first] = pltpu.make_async_copy(source.at[rows], target.at[rows], arrived.at[step])
        copies[first].start()
    return copies


def lane_index(shape):
    return lax.broadcasted_iota(jnp.int32, shape, 1)


def parity():
    return lax.rem(lax.axis_index("tm"), 2)


def in_vmem():
    return pl.BlockSpec(memory_space=pltpu.VMEM)


def in_hbm():
    return pl.BlockSpec(memory_space=pltpu.HBM)


def spread_kernel(codes_hbm, signal_hbm, filters_hbm, near_ref, far_ref, codes_ref, signal_ref, filters_ref, shear_ref, arrived, small):
    chans, count, local_len = codes_ref.shape
    taps = filters_ref.shape[1]
    filters_in = pltpu.make_async_copy(filters_hbm, filters_ref, small.at[0])
    signal_in = pltpu.make_async_copy(signal_hbm, signal_ref, small.at[1])
    filters_in.start()
    fetches = fetch_parts(codes_hbm, codes_ref, arrived, chunk_starts(chans))
    signal_in.start()
    filters_in.wait()
    dict_t = filters_ref[...].T.astype(BF16)
    early, late = dict_t[:LANES], dict_t[LANES:]
    none = jnp.zeros((LANES, count), BF16)
    dict_rows = jnp.concatenate(
        [
            jnp.concatenate([early, none], axis=1),
            jnp.concatenate([late, early], axis=1),
            jnp.concatenate([none, late], axis=1),
        ],
        axis=0,
    )
    lane = lane_index((8, LANES))
    for c in range(0, chans, 2):
        if c in fetches:
            fetches[c].wait()
        pair = [codes_ref[c], codes_ref[c + 1]]
        halves = [jnp.concatenate([x[:, n * LANES : (n + 1) * LANES] for x in pair], axis=1) for n in range(2)]
        terms = jnp.dot(dict_rows, jnp.concatenate(halves, axis=0), preferred_element_type=F32)
        for j in range(2):
            sums = [None] * 4
            for m in range(LANES // 8):
                diagonals = [
                    terms[n * LANES + 8 * m : n * LANES + 8 * m + 8, j * LANES : (j + 1) * LANES] for n in range(3)
                ]
                if m == 0:
                    sums = diagonals + [jnp.zeros((8, LANES), F32)]
                    continue
                turned = [pltpu.roll(d, 8 * m, 1) for d in diagonals]
                inside = lane >= 8 * m
                sums[0] += jnp.where(inside, turned[0], 0.0)
                sums[1] += jnp.where(inside, turned[1], turned[0])
                sums[2] += jnp.where(inside, turned[2], turned[1])
                sums[3] += jnp.where(inside, 0.0, turned[2])
            for n in range(4):
                shear_ref[n, 8 * (c + j) : 8 * (c + j) + 8, :] = sums[n]
    total = jnp.zeros((chans, 4 * LANES), F32)
    for r in range(8):
        row = jnp.concatenate([shear_ref[n, pl.ds(r, chans, stride=8), :] for n in range(4)], axis=1)
        total += pltpu.roll(row, r, 1) if r else row
    signal_in.wait()
    own = total[:, :taps] - signal_ref[...].astype(F32)
    onward = total[:, taps:]
    even = parity() == 0
    near_ref[...] = jnp.where(even, onward, own)
    far_ref[...] = jnp.where(even, own, onward)


def hankel_block(shifted, lane):
    parts = [[], [], []]
    for m in range(LANES // PACK):
        for n in range(3):
            low = shifted[:, n * LANES : (n + 1) * LANES]
            if m:
                high = shifted[:, (n + 1) * LANES : (n + 2) * LANES]
                low = pltpu.roll(jnp.where(lane >= PACK * m, low, high), LANES - PACK * m, 1)
            parts[n].append(low)
    first, second, third = (jnp.concatenate(p, axis=0) for p in parts)
    top = jnp.concatenate([first, second], axis=1)
    bottom = jnp.concatenate([second, third], axis=1)
    return jnp.concatenate([top, bottom], axis=0)


def dict_kernel(codes_hbm, sent_near_ref, sent_far_ref, got_near_ref, got_far_ref, grad_ref, shifted_ref, codes_ref, wide_ref, arrived):
    chans, count, local_len = codes_ref.shape
    fetches = fetch_parts(codes_hbm, codes_ref, arrived, chunk_starts(chans))
    me = lax.axis_index("tm")
    even = lax.rem(me, 2) == 0
    last = me == lax.axis_size("tm") - 1
    own = jnp.where(even, sent_far_ref[...], sent_near_ref[...])
    onward = jnp.where(even, sent_near_ref[...], sent_far_ref[...])
    before = jnp.where(even, got_far_ref[...], got_near_ref[...])
    after = jnp.where(even, got_near_ref[...], got_far_ref[...])
    following = jnp.where(last, 0.0, onward + after)
    error = jnp.concatenate([own + before, following], axis=1).astype(BF16).astype(F32)
    width = error.shape[1]
    for r in range(PACK):
        moved = pltpu.roll(error, width - r, 1) if r else error
        for n in range(4):
            wide_ref[n, pl.ds(r, chans, stride=PACK), :] = moved[:, n * LANES : (n + 1) * LANES]
    lane = lane_index((PACK, LANES))

    total = jnp.zeros(grad_ref.shape, F32)
    for c in range(chans):
        if c in fetches:
            fetches[c].wait()
        rows = pl.ds(c * PACK, PACK)
        shifted = jnp.concatenate([wide_ref[n, rows, :] for n in range(4)], axis=1).astype(BF16)
        shifted_ref[c] = shifted
        total += jnp.dot(codes_ref[c], hankel_block(shifted, lane), preferred_element_type=F32)
    grad_ref[...] = total


def codes_kernel(first, after_ref, codes_hbm, shifted_ref, filters_ref, *refs):
    new_hbm, codes_ref, new_ref, arrived, left = refs[-5:]
    chans, count, local_len = codes_ref.shape
    starts = [0, chans // 4, chans]
    fetches = fetch_parts(codes_hbm.at[pl.ds(first, chans)], codes_ref, arrived, starts)
    dict_b = filters_ref[...].astype(BF16)
    lane = lane_index((PACK, LANES))
    stores = []
    done = 0
    for c in range(chans):
        grad = jnp.dot(dict_b, hankel_block(shifted_ref[first + c], lane), preferred_element_type=F32)
        if c in fetches:
            fetches[c].wait()
        moved = codes_ref[c].astype(F32) - ETA_CODE * grad
        new_ref[c] = (moved - jnp.clip(moved, -LAM, LAM)).astype(BF16)
        if c + 1 == chans or (c + 1) % GROUP == 0:
            rows = pl.ds(done, c + 1 - done)
            target = new_hbm.at[pl.ds(first + done, c + 1 - done)]
            stores.append(pltpu.make_async_copy(new_ref.at[rows], target, left.at[len(stores)]))
            stores[-1].start()
            done = c + 1
    for store in stores:
        store.wait()


def step_codes(first, chans, after, codes, shifted, filters, partial):
    count, local_len = codes.shape[1:]
    earlier = [] if partial is None else [pltpu.with_memory_space_constraint(partial, pltpu.HBM)]
    return pl.pallas_call(
        functools.partial(codes_kernel, first),
        in_specs=[in_vmem(), in_hbm(), in_vmem(), in_vmem()] + [in_hbm() for _ in earlier],
        out_specs=in_hbm(),
        out_shape=pltpu.HBM(codes.shape, BF16),
        scratch_shapes=[
            pltpu.VMEM((chans, count, local_len), BF16),
            pltpu.VMEM((chans, count, local_len), BF16),
            pltpu.SemaphoreType.DMA((2,)),
            pltpu.SemaphoreType.DMA((-(-chans // GROUP),)),
        ],
        input_output_aliases={4: 0} if earlier else {},
        compiler_params=pltpu.CompilerParams(vmem_limit_bytes=VMEM_BYTES),
        cost_estimate=pl.CostEstimate(
            flops=2 * chans * count * local_len * shifted.shape[2] // 2,
            bytes_accessed=4 * chans * count * local_len,
            transcendentals=0,
        ),
        name="codes_step",
    )(after, pltpu.with_memory_space_constraint(codes, pltpu.HBM), shifted, filters, *earlier)


def normalize_kernel(scale, new_hbm, total_ref, last_ref, filters_ref, out_ref):
    half = out_ref.shape[0]
    rows = pl.ds(pl.multiple_of(parity() * half, 8), half)
    stepped = filters_ref[rows, :] - ETA_FILT * ((total_ref[...] + last_ref[...]) / scale)
    out_ref[...] = stepped / jnp.sqrt(jnp.sum(stepped * stepped, axis=1, keepdims=True) + EPS)


def exchange(block, distance):
    size = lax.axis_size("tm")
    return lax.ppermute(block, "tm", [(i, i ^ distance) for i in range(size)])


def shards(signal, codes, filters):
    chans, count, local_len = codes.shape
    taps = filters.shape[1]
    devices = lax.axis_size("tm")
    params = pltpu.CompilerParams(vmem_limit_bytes=VMEM_BYTES)
    halo = jax.ShapeDtypeStruct((chans, taps), F32)
    matmul_flops = 2 * chans * count * local_len * taps
    sent_near, sent_far = pl.pallas_call(
        spread_kernel,
        in_specs=[in_hbm()] * 3,
        out_specs=[in_vmem()] * 2,
        out_shape=[halo, halo],
        scratch_shapes=[
            pltpu.VMEM(codes.shape, BF16),
            pltpu.VMEM(signal.shape, BF16),
            pltpu.VMEM(filters.shape, F32),
            pltpu.VMEM((4, 8 * chans, LANES), F32),
            pltpu.SemaphoreType.DMA((CHUNKS,)),
            pltpu.SemaphoreType.DMA((2,)),
        ],
        compiler_params=params,
        cost_estimate=pl.CostEstimate(flops=matmul_flops, bytes_accessed=codes.size * 2, transcendentals=0),
        name="spread",
    )(*(pltpu.with_memory_space_constraint(a, pltpu.HBM) for a in (codes, signal, filters)))

    across = [(i, i + 1) for i in range(1, devices - 1, 2)]
    across += [(j, i) for i, j in across]
    got_near = exchange(sent_near, 1)
    got_far = lax.ppermute(sent_far, "tm", across)

    terms, shifted = pl.pallas_call(
        dict_kernel,
        in_specs=[in_hbm()] + [in_vmem()] * 4,
        out_specs=[in_vmem()] * 2,
        out_shape=[
            jax.ShapeDtypeStruct((count, taps), F32),
            jax.ShapeDtypeStruct((chans, PACK, 2 * taps), BF16),
        ],
        scratch_shapes=[
            pltpu.VMEM(codes.shape, BF16),
            pltpu.VMEM((4, chans * PACK, LANES), F32),
            pltpu.SemaphoreType.DMA((CHUNKS,)),
        ],
        compiler_params=params,
        cost_estimate=pl.CostEstimate(flops=matmul_flops, bytes_accessed=codes.size * 2, transcendentals=0),
        name="dict_grad",
    )(pltpu.with_memory_space_constraint(codes, pltpu.HBM), sent_near, sent_far, got_near, got_far)

    half = count // 2
    core = parity()
    total = lax.dynamic_slice_in_dim(terms, core * half, half, 0)
    total += exchange(lax.dynamic_slice_in_dim(terms, (1 - core) * half, half, 0), 1)
    distances = [2]
    while 2 * distances[-1] < devices:
        distances.append(2 * distances[-1])
    new_codes, first = None, 0
    for place, distance in enumerate(distances):
        received = exchange(total, distance)
        end = chans * (place + 1) // len(distances)
        new_codes = step_codes(first, end - first, total, codes, shifted, filters, new_codes)
        first = end
        if distance != distances[-1]:
            total += received
    mine = pl.pallas_call(
        functools.partial(normalize_kernel, float(chans * local_len * devices)),
        in_specs=[in_hbm(), in_vmem(), in_vmem(), in_vmem()],
        out_specs=in_vmem(),
        out_shape=jax.ShapeDtypeStruct((half, taps), F32),
        compiler_params=params,
        name="normalize",
    )(pltpu.with_memory_space_constraint(new_codes, pltpu.HBM), total, received, filters)
    other = exchange(mine, 1)
    lower = core == 0
    new_filters = jnp.concatenate([jnp.where(lower, mine, other), jnp.where(lower, other, mine)], axis=0)
    return (new_codes, new_filters)


def solution(mesh):
    return jax.shard_map(
        shards,
        mesh=mesh,
        in_specs=(P("groups", "tm"), P("groups", None, "tm"), P()),
        out_specs=(P("groups", None, "tm"), P("groups", None)),
        check_vma=False,
    )
```

time: 949 us -> 39.7 us (0.04)
  local copies, waits for them, and re-layouts: 772 us -> 0.02 us
  waiting for transfers between devices: 71.3 us -> 4.99 us
  matrix products: 50.4 us -> 0 us
  other arithmetic: 32.4 us -> 0.71 us
  Pallas kernels: 0 us -> 18.7 us
  between operations: 14.2 us -> 0.76 us
    gather x4 -> x0, local copies, waits for them, and re-layouts: 750 us -> none  [the longest x2 498 us: toeplitz(): return jnp.take(padded, lookup, axis=1)]
    psum x1 -> x0, waiting for transfers between devices: 69.5 us -> none  [shards(): summed = lax.psum(grad_terms, 'tm')]
    dot_general x4 -> x0, matrix products: 50.4 us -> none  [the longest x1 18 us: local_step(): jnp.einsum('cns,kts->cknt', extended, table, preferred_element_type=jnp.f...]
    select_n x1, other arithmetic: 22.9 us -> 0.01 us  [shards(): jnp.where(lower, mine, other)]
    pallas_call x0 -> x6, Pallas kernels: none -> 18.7 us  [the longest x3 8.74 us: step_codes(): pl.pallas_call(functools.partial(codes_kernel, first), in_specs=[in_vmem(...]
    unnamed x14 -> x2, local copies, waits for them, and re-layouts: 12.5 us -> 0.01 us
  transfers between devices with their start and end apart: 3 -> 7, of which waited for: 2 -> 4; matrix products, arithmetic and copies ran while one was open for 59% -> 0% of each run, Pallas kernels for 0% -> 22%
where the time goes in v1:
time: 39.7 us; the launch traced here: 39.5 us
  Pallas kernels  18.7 us (47%)
  starting transfers between devices  14.4 us (36%)
  waiting for transfers between devices  4.99 us (13%)
  between operations  0.76 us (2%)
  other arithmetic  0.71 us (2%)
    ppermute x6, starting transfers between devices, exchange(): return lax.ppermute(block, 'tm', [(i, i ^ distance) for i in range(size)])  13.7 us
    pallas_call x3, Pallas kernels, step_codes(): pl.pallas_call(functools.partial(codes_kernel, first), in_specs=[in_vmem(...  8.74 us
    pallas_call x1, Pallas kernels, shards(): pl.pallas_call(spread_kernel, in_specs=[in_hbm()] * 3, out_specs=[in_vmem...  5.86 us
    ppermute x6, waiting for transfers between devices, exchange(): return lax.ppermute(block, 'tm', [(i, i ^ distance) for i in range(size)])  4.99 us
    pallas_call x1, Pallas kernels, shards(): pl.pallas_call(dict_kernel, in_specs=[in_hbm()] + [in_vmem()] * 4, out_sp...  3.95 us
  transfers between devices with their start and end apart: 7, of which 4 were waited for; matrix products, arithmetic and copies ran while one was open for 0% of the time, Pallas kernels for 22%

profile of v1, /device:TPU:0, one launch (start us, length us, event | category | flops | bytes accessed | tf_op | source)
XLA Modules:
  0.0 39.5 jit_solution(13354104340050576172)
XLA Ops:
  0.6 0.0 copy-start
  0.6 5.9 %spread.1 = (f32[64,256]{1,0:T(8,128)S(1)}, f32[64,256]{1,0:T(8,128)S(1)}) custom-call(bf16[64,128,256]{2,1,0:T(8,128)(2,1)} %codes_hbm.9, bf16[64,256]{1,0:T(8,128)(2,1)} %signal_hbm.1, f32[128,256]{1,0:T(8,128)} %filters_ref.7), custom_call_target="tpu_custom_call" | custom-call | flops 1073741824 | bytes 4194304 | tf_op jit(solution)/shard_map/spread/pallas_call | solution.py:223
  6.5 0.5 %collective-permute-start = (f32[64,256]{1,0:T(8,128)S(1)}, f32[64,256]{1,0:T(8,128)S(1)}, u32[]{:S(2)}, u32[]{:S(2)}) collective-permute-start(f32[64,256]{1,0:T(8,128)S(1)} %get-tuple-element.6.sent_near_ref), channel_id=1, source_target_pairs={{0,1},{1,0},{2,3},{3,2},{4,5},{5,4},{6,7},{7,6},{8,9},{9,8},{10,11... | collective-permute-start | bytes 196616 | tf_op jit(solution)/shard_map/ppermute | solution.py:213
  7.0 0.7 %collective-permute-start.1 = (f32[64,256]{1,0:T(8,128)S(1)}, f32[64,256]{1,0:T(8,128)S(1)}, u32[]{:S(2)}, u32[]{:S(2)}) collective-permute-start(f32[64,256]{1,0:T(8,128)S(1)} %get-tuple-element.7.sent_far_ref), channel_id=1, source_target_pairs={{1,2},{3,4},{5,6},{7,8},{9,10},{11,12},{13,14},{2,1},{4,3},{6,5},{... | collective-permute-start | bytes 196616 | tf_op jit(solution)/shard_map/ppermute | solution.py:244
  7.7 0.2 collective-permute-done.got_near_ref
  8.0 0.0 collective-permute-done.1.got_far_ref
  8.0 4.0 %dict_grad.1 = (f32[128,256]{1,0:T(8,128)S(1)}, bf16[64,16,512]{2,1,0:T(8,128)(2,1)S(1)}) custom-call(bf16[64,128,256]{2,1,0:T(8,128)(2,1)} %codes_hbm.9, f32[64,256]{1,0:T(8,128)S(1)} %get-tuple-element.6.sent_near_ref, f32[64,256]{1,0:T(8,128)S(1)} %get-tuple-element.7.sent_far_ref, f32[64,256]{1,0:T(8,128)S(1)} %collective-permute-done.got_near_ref, ...), custom_call_target="tpu_custom_call" | custom-call | flops 1073741824 | bytes 4194304 | tf_op jit(solution)/shard_map/dict_grad/pallas_call | solution.py:246
  11.9 5.6 %collective-permute-start.2 = (f32[64,256]{1,0:T(8,128)S(1)}, f32[64,256]{1,0:T(8,128)S(1)}, u32[]{:S(2)}, u32[]{:S(2)}) collective-permute-start(f32[64,256]{1,0:T(8,128)S(1)} %constant_dynamic-slice_fusion), channel_id=1, source_target_pairs={{0,1},{1,0},{2,3},{3,2},{4,5},{5,4},{6,7},{7,6},{8,9},{9,8},{10,11... | collective-permute-start | bytes 196616 | tf_op jit(solution)/shard_map/ppermute | solution.py:213
  17.6 0.9 %collective-permute-done.2 = f32[64,256]{1,0:T(8,128)S(1)} collective-permute-done((f32[64,256]{1,0:T(8,128)S(1)}, f32[64,256]{1,0:T(8,128)S(1)}, u32[]{:S(2)}, u32[]{:S(2)}) %collective-permute-start.2) | collective-permute-done | bytes 65568 | tf_op jit(solution)/shard_map/ppermute | solution.py:213
  18.5 3.1 %collective-permute-start.3 = (f32[64,256]{1,0:T(8,128)S(1)}, f32[64,256]{1,0:T(8,128)S(1)}, u32[]{:S(2)}, u32[]{:S(2)}) collective-permute-start(f32[64,256]{1,0:T(8,128)S(1)} %dynamic-slice_add_fusion.after_ref), channel_id=1, source_target_pairs={{0,2},{1,3},{2,0},{3,1},{4,6},{5,7},{6,4},{7,5},{8,10},{9,11},{10,... | collective-permute-start | bytes 196616 | tf_op jit(solution)/shard_map/ppermute | solution.py:213
  21.6 2.6 %collective-permute-done.3 = f32[64,256]{1,0:T(8,128)S(1)} collective-permute-done((f32[64,256]{1,0:T(8,128)S(1)}, f32[64,256]{1,0:T(8,128)S(1)}, u32[]{:S(2)}, u32[]{:S(2)}) %collective-permute-start.3) | collective-permute-done | bytes 65568 | tf_op jit(solution)/shard_map/ppermute | solution.py:213
  24.2 1.8 %collective-permute-start.4 = (f32[64,256]{1,0:T(8,128)S(1)}, f32[64,256]{1,0:T(8,128)S(1)}, u32[]{:S(2)}, u32[]{:S(2)}) collective-permute-start(f32[64,256]{1,0:T(8,128)S(1)} %add.18.after_ref), channel_id=1, source_target_pairs={{0,4},{1,5},{2,6},{3,7},{4,0},{5,1},{6,2},{7,3},{8,12},{9,13},{10,... | collective-permute-start | bytes 196616 | tf_op jit(solution)/shard_map/ppermute | solution.py:213
  25.9 0.0 copy-done
  25.9 2.9 %codes_step.3.refs_0_ = bf16[64,128,256]{2,1,0:T(8,128)(2,1)} custom-call(f32[64,256]{1,0:T(8,128)S(1)} %dynamic-slice_add_fusion.after_ref, bf16[64,128,256]{2,1,0:T(8,128)(2,1)} %codes_hbm.9, bf16[64,16,512]{2,1,0:T(8,128)(2,1)S(1)} %get-tuple-element.9.shifted_ref, f32[128,256]{1,0:T(8,128)S(1)} %copy-done), custom_call_target="tpu_custom_call" | custom-call | flops 352321536 | bytes 2752512 | tf_op jit(solution)/shard_map/codes_step/pallas_call | solution.py:182
  28.8 0.0 collective-permute-done.4
  28.9 2.6 %collective-permute-start.5 = (f32[64,256]{1,0:T(8,128)S(1)}, f32[64,256]{1,0:T(8,128)S(1)}, u32[]{:S(2)}, u32[]{:S(2)}) collective-permute-start(f32[64,256]{1,0:T(8,128)S(1)} %add.19.after_ref.total_ref), channel_id=1, source_target_pairs={{0,8},{1,9},{2,10},{3,11},{4,12},{5,13},{6,14},{7,15},{8,0},{9,1},... | collective-permute-start | bytes 196616 | tf_op jit(solution)/shard_map/ppermute | solution.py:213
  31.5 2.9 %codes_step.4.refs_0_ = bf16[64,128,256]{2,1,0:T(8,128)(2,1)} custom-call(f32[64,256]{1,0:T(8,128)S(1)} %add.18.after_ref, bf16[64,128,256]{2,1,0:T(8,128)(2,1)} %codes_hbm.9, bf16[64,16,512]{2,1,0:T(8,128)(2,1)S(1)} %get-tuple-element.9.shifted_ref, f32[128,256]{1,0:T(8,128)S(1)} %copy-done, ...), custom_call_target="tpu_custom_call", output_to_operand_aliasing={{}: (4, {})} | custom-call | flops 352321536 | bytes 2752512 | tf_op jit(solution)/shard_map/codes_step/pallas_call | solution.py:182
  34.4 3.0 %codes_step.5.new_hbm = bf16[64,128,256]{2,1,0:T(8,128)(2,1)} custom-call(f32[64,256]{1,0:T(8,128)S(1)} %add.19.after_ref.total_ref, bf16[64,128,256]{2,1,0:T(8,128)(2,1)} %codes_hbm.9, bf16[64,16,512]{2,1,0:T(8,128)(2,1)S(1)} %get-tuple-element.9.shifted_ref, f32[128,256]{1,0:T(8,128)S(1)} %copy-done, ...), custom_call_target="tpu_custom_call", output_to_operand_aliasing={{}: (4, {})} | custom-call | flops 369098752 | bytes 2883584 | tf_op jit(solution)/shard_map/codes_step/pallas_call | solution.py:182
  37.4 0.0 collective-permute-done.5.last_ref
  37.4 0.1 normalize.1
  37.5 0.1 collective-permute-start.6
  37.6 1.2 %collective-permute-done.6 = f32[64,256]{1,0:T(8,128)S(1)} collective-permute-done((f32[64,256]{1,0:T(8,128)S(1)}, f32[64,256]{1,0:T(8,128)S(1)}, u32[]{:S(2)}, u32[]{:S(2)}) %collective-permute-start.6) | collective-permute-done | bytes 65568 | tf_op jit(solution)/shard_map/ppermute | solution.py:213
  38.9 0.7 %pad_maximum_fusion = f32[128,256]{1,0:T(8,128)} fusion(f32[64,256]{1,0:T(8,128)S(1)} %get-tuple-element.11, f32[64,256]{1,0:T(8,128)S(1)} %get-tuple-element.10), kind=kLoop, calls=%fused_computation | loop fusion | flops 32768 | bytes 262144 | tf_op jit(solution)/shard_map/concatenate | solution.py:289
  (5 shorter events, 0.1 us)
Async XLA Ops:
  0.6 25.3 %copy-start = (f32[128,256]{1,0:T(8,128)S(1)}, f32[128,256]{1,0:T(8,128)}, u32[]{:S(2)}) copy-start(f32[128,256]{1,0:T(8,128)} %filters_ref.7) | copy-start | bytes 393220
  6.5 1.4 %collective-permute-start = (f32[64,256]{1,0:T(8,128)S(1)}, f32[64,256]{1,0:T(8,128)S(1)}, u32[]{:S(2)}, u32[]{:S(2)}) collective-permute-start(f32[64,256]{1,0:T(8,128)S(1)} %get-tuple-element.6.sent_near_ref), channel_id=1, source_target_pairs={{0,1},{1,0},{2,3},{3,2},{4,5},{5,4},{6,7},{7,6},{8,9},{9,8},{10,11... | collective-permute-start | bytes 196616 | tf_op jit(solution)/shard_map/ppermute | solution.py:213
  7.0 0.9 %collective-permute-start.1 = (f32[64,256]{1,0:T(8,128)S(1)}, f32[64,256]{1,0:T(8,128)S(1)}, u32[]{:S(2)}, u32[]{:S(2)}) collective-permute-start(f32[64,256]{1,0:T(8,128)S(1)} %get-tuple-element.7.sent_far_ref), channel_id=1, source_target_pairs={{1,2},{3,4},{5,6},{7,8},{9,10},{11,12},{13,14},{2,1},{4,3},{6,5},{... | collective-permute-start | bytes 196616 | tf_op jit(solution)/shard_map/ppermute | solution.py:244
  11.9 6.5 %collective-permute-start.2 = (f32[64,256]{1,0:T(8,128)S(1)}, f32[64,256]{1,0:T(8,128)S(1)}, u32[]{:S(2)}, u32[]{:S(2)}) collective-permute-start(f32[64,256]{1,0:T(8,128)S(1)} %constant_dynamic-slice_fusion), channel_id=1, source_target_pairs={{0,1},{1,0},{2,3},{3,2},{4,5},{5,4},{6,7},{7,6},{8,9},{9,8},{10,11... | collective-permute-start | bytes 196616 | tf_op jit(solution)/shard_map/ppermute | solution.py:213
  18.5 5.7 %collective-permute-start.3 = (f32[64,256]{1,0:T(8,128)S(1)}, f32[64,256]{1,0:T(8,128)S(1)}, u32[]{:S(2)}, u32[]{:S(2)}) collective-permute-start(f32[64,256]{1,0:T(8,128)S(1)} %dynamic-slice_add_fusion.after_ref), channel_id=1, source_target_pairs={{0,2},{1,3},{2,0},{3,1},{4,6},{5,7},{6,4},{7,5},{8,10},{9,11},{10,... | collective-permute-start | bytes 196616 | tf_op jit(solution)/shard_map/ppermute | solution.py:213
  24.2 4.7 %collective-permute-start.4 = (f32[64,256]{1,0:T(8,128)S(1)}, f32[64,256]{1,0:T(8,128)S(1)}, u32[]{:S(2)}, u32[]{:S(2)}) collective-permute-start(f32[64,256]{1,0:T(8,128)S(1)} %add.18.after_ref), channel_id=1, source_target_pairs={{0,4},{1,5},{2,6},{3,7},{4,0},{5,1},{6,2},{7,3},{8,12},{9,13},{10,... | collective-permute-start | bytes 196616 | tf_op jit(solution)/shard_map/ppermute | solution.py:213
  28.9 8.5 %collective-permute-start.5 = (f32[64,256]{1,0:T(8,128)S(1)}, f32[64,256]{1,0:T(8,128)S(1)}, u32[]{:S(2)}, u32[]{:S(2)}) collective-permute-start(f32[64,256]{1,0:T(8,128)S(1)} %add.19.after_ref.total_ref), channel_id=1, source_target_pairs={{0,8},{1,9},{2,10},{3,11},{4,12},{5,13},{6,14},{7,15},{8,0},{9,1},... | collective-permute-start | bytes 196616 | tf_op jit(solution)/shard_map/ppermute | solution.py:213
  37.5 1.3 %collective-permute-start.6 = (f32[64,256]{1,0:T(8,128)S(1)}, f32[64,256]{1,0:T(8,128)S(1)}, u32[]{:S(2)}, u32[]{:S(2)}) collective-permute-start(f32[64,256]{1,0:T(8,128)S(1)} %normalize.1), channel_id=1, source_target_pairs={{0,1},{1,0},{2,3},{3,2},{4,5},{5,4},{6,7},{7,6},{8,9},{9,8},{10,11... | collective-permute-start | bytes 196616 | tf_op jit(solution)/shard_map/ppermute | solution.py:213

commit v2 on v1

--- a/solution.py
+++ b/solution.py
@@ -14,15 +14,16 @@
 
 F32 = jnp.float32
 BF16 = jnp.bfloat16
+HOP = BF16
 LANES = 128
 GROUP = 8
-CHUNKS = 4
+CHUNKS = 3
 PACK = 16
-VMEM_BYTES = 16 << 20
+VMEM_BYTES = 5 << 20
 
 
 def chunk_starts(chans):
-    return [0, chans // 8, chans // 4, chans // 2, chans]
+    return [0, chans // 8, 3 * chans // 8, chans]
 
 
 def fetch_parts(source, target, arrived, starts):
@@ -50,7 +51,7 @@
     return pl.BlockSpec(memory_space=pltpu.HBM)
 
 
-def spread_kernel(codes_hbm, signal_hbm, filters_hbm, near_ref, far_ref, codes_ref, signal_ref, filters_ref, shear_ref, arrived, small):
+def spread_kernel(codes_hbm, signal_hbm, filters_hbm, codes_ref, near_ref, far_ref, signal_ref, filters_ref, shear_ref, arrived, small):
     chans, count, local_len = codes_ref.shape
     taps = filters_ref.shape[1]
     filters_in = pltpu.make_async_copy(filters_hbm, filters_ref, small.at[0])
@@ -121,9 +122,8 @@
     return jnp.concatenate([top, bottom], axis=0)
 
 
-def dict_kernel(codes_hbm, sent_near_ref, sent_far_ref, got_near_ref, got_far_ref, grad_ref, shifted_ref, codes_ref, wide_ref, arrived):
+def dict_kernel(codes_ref, sent_near_ref, sent_far_ref, got_near_ref, got_far_ref, mine_ref, other_ref, shifted_ref, wide_ref):
     chans, count, local_len = codes_ref.shape
-    fetches = fetch_parts(codes_hbm, codes_ref, arrived, chunk_starts(chans))
     me = lax.axis_index("tm")
     even = lax.rem(me, 2) == 0
     last = me == lax.axis_size("tm") - 1
@@ -140,31 +140,28 @@
             wide_ref[n, pl.ds(r, chans, stride=PACK), :] = moved[:, n * LANES : (n + 1) * LANES]
     lane = lane_index((PACK, LANES))
 
-    total = jnp.zeros(grad_ref.shape, F32)
+    total = jnp.zeros((count, error.shape[1] // 2), F32)
     for c in range(chans):
-        if c in fetches:
-            fetches[c].wait()
         rows = pl.ds(c * PACK, PACK)
         shifted = jnp.concatenate([wide_ref[n, rows, :] for n in range(4)], axis=1).astype(BF16)
         shifted_ref[c] = shifted
         total += jnp.dot(codes_ref[c], hankel_block(shifted, lane), preferred_element_type=F32)
-    grad_ref[...] = total
-
-
-def codes_kernel(first, after_ref, codes_hbm, shifted_ref, filters_ref, *refs):
-    new_hbm, codes_ref, new_ref, arrived, left = refs[-5:]
-    chans, count, local_len = codes_ref.shape
-    starts = [0, chans // 4, chans]
-    fetches = fetch_parts(codes_hbm.at[pl.ds(first, chans)], codes_ref, arrived, starts)
+    half = count // 2
+    mine_ref[...] = jnp.where(even, total[:half], total[half:])
+    other_ref[...] = jnp.where(even, total[half:], total[:half])
+
+
+def codes_kernel(first, sum_ref, codes_ref, shifted_ref, filters_ref, *refs):
+    new_hbm, kept_ref, new_ref, left = refs[-4:]
+    kept_ref[...] = sum_ref[...]
+    chans = new_ref.shape[0]
     dict_b = filters_ref[...].astype(BF16)
     lane = lane_index((PACK, LANES))
     stores = []
     done = 0
     for c in range(chans):
         grad = jnp.dot(dict_b, hankel_block(shifted_ref[first + c], lane), preferred_element_type=F32)
-        if c in fetches:
-            fetches[c].wait()
-        moved = codes_ref[c].astype(F32) - ETA_CODE * grad
+        moved = codes_ref[first + c].astype(F32) - ETA_CODE * grad
         new_ref[c] = (moved - jnp.clip(moved, -LAM, LAM)).astype(BF16)
         if c + 1 == chans or (c + 1) % GROUP == 0:
             rows = pl.ds(done, c + 1 - done)
@@ -176,18 +173,19 @@
         store.wait()
 
 
-def step_codes(first, chans, after, codes, shifted, filters, partial):
+def step_codes(first, chans, total, codes, shifted, filters, partial):
     count, local_len = codes.shape[1:]
     earlier = [] if partial is None else [pltpu.with_memory_space_constraint(partial, pltpu.HBM)]
     return pl.pallas_call(
         functools.partial(codes_kernel, first),
-        in_specs=[in_vmem(), in_hbm(), in_vmem(), in_vmem()] + [in_hbm() for _ in earlier],
-        out_specs=in_hbm(),
-        out_shape=pltpu.HBM(codes.shape, BF16),
+        in_specs=[in_vmem()] * 4 + [in_hbm() for _ in earlier],
+        out_specs=[in_hbm(), in_vmem()],
+        out_shape=[
+            pltpu.HBM(codes.shape, BF16),
+            jax.ShapeDtypeStruct(total.shape, total.dtype),
+        ],
         scratch_shapes=[
             pltpu.VMEM((chans, count, local_len), BF16),
-            pltpu.VMEM((chans, count, local_len), BF16),
-            pltpu.SemaphoreType.DMA((2,)),
             pltpu.SemaphoreType.DMA((-(-chans // GROUP),)),
         ],
         input_output_aliases={4: 0} if earlier else {},
@@ -198,14 +196,22 @@
             transcendentals=0,
         ),
         name="codes_step",
-    )(after, pltpu.with_memory_space_constraint(codes, pltpu.HBM), shifted, filters, *earlier)
-
-
-def normalize_kernel(scale, new_hbm, total_ref, last_ref, filters_ref, out_ref):
+    )(total, codes, shifted, filters, *earlier)
+
+
+def normalize_kernel(scale, total_ref, last_ref, filters_ref, out_ref):
     half = out_ref.shape[0]
     rows = pl.ds(pl.multiple_of(parity() * half, 8), half)
-    stepped = filters_ref[rows, :] - ETA_FILT * ((total_ref[...] + last_ref[...]) / scale)
+    total = total_ref[...].astype(F32) + last_ref[...].astype(F32)
+    stepped = filters_ref[rows, :] - ETA_FILT * (total / scale)
     out_ref[...] = stepped / jnp.sqrt(jnp.sum(stepped * stepped, axis=1, keepdims=True) + EPS)
+
+
+def join_kernel(mine_ref, other_ref, out_ref):
+    half = mine_ref.shape[0]
+    even = parity() == 0
+    out_ref[:half, :] = jnp.where(even, mine_ref[...], other_ref[...])
+    out_ref[half:, :] = jnp.where(even, other_ref[...], mine_ref[...])
 
 
 def exchange(block, distance):
@@ -217,16 +223,16 @@
     chans, count, local_len = codes.shape
     taps = filters.shape[1]
     devices = lax.axis_size("tm")
+    half = count // 2
     params = pltpu.CompilerParams(vmem_limit_bytes=VMEM_BYTES)
     halo = jax.ShapeDtypeStruct((chans, taps), F32)
     matmul_flops = 2 * chans * count * local_len * taps
-    sent_near, sent_far = pl.pallas_call(
+    held, sent_near, sent_far = pl.pallas_call(
         spread_kernel,
         in_specs=[in_hbm()] * 3,
-        out_specs=[in_vmem()] * 2,
-        out_shape=[halo, halo],
+        out_specs=[in_vmem()] * 3,
+        out_shape=[jax.ShapeDtypeStruct(codes.shape, BF16), halo, halo],
         scratch_shapes=[
-            pltpu.VMEM(codes.shape, BF16),
             pltpu.VMEM(signal.shape, BF16),
             pltpu.VMEM(filters.shape, F32),
             pltpu.VMEM((4, 8 * chans, LANES), F32),
@@ -243,50 +249,49 @@
     got_near = exchange(sent_near, 1)
     got_far = lax.ppermute(sent_far, "tm", across)
 
-    terms, shifted = pl.pallas_call(
+    mine, other, shifted = pl.pallas_call(
         dict_kernel,
-        in_specs=[in_hbm()] + [in_vmem()] * 4,
-        out_specs=[in_vmem()] * 2,
+        in_specs=[in_vmem()] * 5,
+        out_specs=[in_vmem()] * 3,
         out_shape=[
-            jax.ShapeDtypeStruct((count, taps), F32),
+            jax.ShapeDtypeStruct((half, taps), F32),
+            jax.ShapeDtypeStruct((half, taps), F32),
             jax.ShapeDtypeStruct((chans, PACK, 2 * taps), BF16),
         ],
-        scratch_shapes=[
-            pltpu.VMEM(codes.shape, BF16),
-            pltpu.VMEM((4, chans * PACK, LANES), F32),
-            pltpu.SemaphoreType.DMA((CHUNKS,)),
-        ],
+        scratch_shapes=[pltpu.VMEM((4, chans * PACK, LANES), F32)],
         compiler_params=params,
         cost_estimate=pl.CostEstimate(flops=matmul_flops, bytes_accessed=codes.size * 2, transcendentals=0),
         name="dict_grad",
-    )(pltpu.with_memory_space_constraint(codes, pltpu.HBM), sent_near, sent_far, got_near, got_far)
-
-    half = count // 2
-    core = parity()
-    total = lax.dynamic_slice_in_dim(terms, core * half, half, 0)
-    total += exchange(lax.dynamic_slice_in_dim(terms, (1 - core) * half, half, 0), 1)
+    )(held, sent_near, sent_far, got_near, got_far)
+
+    total = mine + exchange(other, 1)
     distances = [2]
     while 2 * distances[-1] < devices:
         distances.append(2 * distances[-1])
     new_codes, first = None, 0
     for place, distance in enumerate(distances):
-        received = exchange(total, distance)
+        sent = total.astype(HOP)
+        received = exchange(sent, distance)
         end = chans * (place + 1) // len(distances)
-        new_codes = step_codes(first, end - first, total, codes, shifted, filters, new_codes)
+        new_codes, kept = step_codes(first, end - first, sent, held, shifted, filters, new_codes)
         first = end
-        if distance != distances[-1]:
-            total += received
+        total = kept.astype(F32) + received.astype(F32)
     mine = pl.pallas_call(
         functools.partial(normalize_kernel, float(chans * local_len * devices)),
-        in_specs=[in_hbm(), in_vmem(), in_vmem(), in_vmem()],
+        in_specs=[in_vmem()] * 3,
         out_specs=in_vmem(),
         out_shape=jax.ShapeDtypeStruct((half, taps), F32),
         compiler_params=params,
         name="normalize",
-    )(pltpu.with_memory_space_constraint(new_codes, pltpu.HBM), total, received, filters)
-    other = exchange(mine, 1)
-    lower = core == 0
-    new_filters = jnp.concatenate([jnp.where(lower, mine, other), jnp.where(lower, other, mine)], axis=0)
+    )(kept, received, filters)
+    new_filters = pl.pallas_call(
+        join_kernel,
+        in_specs=[in_vmem()] * 2,
+        out_specs=in_vmem(),
+        out_shape=jax.ShapeDtypeStruct((count, taps), F32),
+        compiler_params=params,
+        name="join",
+    )(mine, exchange(mine, 1))
     return (new_codes, new_filters)
 
 

time: 39.7 us -> 33.2 us (0.84)
  Pallas kernels: 18.7 us -> 14.5 us
  waiting for transfers between devices: 4.99 us -> 2.63 us
  starting transfers between devices: 14.4 us -> 15.2 us
  other arithmetic: 0.71 us -> 0.03 us
    pallas_call x3, Pallas kernels: 8.74 us -> 5.42 us  [step_codes(): pl.pallas_call(functools.partial(codes_kernel, first), in_specs=[in_vmem(...]
    ppermute x6, waiting for transfers between devices: 4.99 us -> 2.63 us  [exchange(): return lax.ppermute(block, 'tm', [(i, i ^ distance) for i in range(size)])]
    ppermute x6, starting transfers between devices: 13.7 us -> 14.5 us  [exchange(): return lax.ppermute(block, 'tm', [(i, i ^ distance) for i in range(size)])]
    concatenate x1 -> x0, other arithmetic: 0.67 us -> none  [shards(): jnp.concatenate([jnp.where(lower, mine, other), jnp.where(lower, other, m...]
    pallas_call x1, Pallas kernels: 5.86 us -> 5.38 us  [shards(): pl.pallas_call(spread_kernel, in_specs=[in_hbm()] * 3, out_specs=[in_vmem...]
    pallas_call x1 -> x2, Pallas kernels: 3.95 us -> 3.62 us  [the longest x1 2.95 us: shards(): pl.pallas_call(dict_kernel, in_specs=[in_vmem()] * 5, out_specs=[in_vmem(...]
  transfers between devices with their start and end apart: 7 -> 7, of which waited for: 4 -> 6; matrix products, arithmetic and copies ran while one was open for 0% -> 0% of each run, Pallas kernels for 22% -> 16%
where the time goes in v2:
time: 33.2 us; the launch traced here: 33.1 us
  starting transfers between devices  15.2 us (46%)
  Pallas kernels  14.5 us (44%)
  waiting for transfers between devices  2.63 us (8%)
  between operations  0.71 us (2%)
    ppermute x6, starting transfers between devices, exchange(): return lax.ppermute(block, 'tm', [(i, i ^ distance) for i in range(size)])  14.5 us
    pallas_call x3, Pallas kernels, step_codes(): pl.pallas_call(functools.partial(codes_kernel, first), in_specs=[in_vmem(...  5.42 us
    pallas_call x1, Pallas kernels, shards(): pl.pallas_call(spread_kernel, in_specs=[in_hbm()] * 3, out_specs=[in_vmem...  5.38 us
    pallas_call x1, Pallas kernels, shards(): pl.pallas_call(dict_kernel, in_specs=[in_vmem()] * 5, out_specs=[in_vmem(...  2.95 us
    ppermute x6, waiting for transfers between devices, exchange(): return lax.ppermute(block, 'tm', [(i, i ^ distance) for i in range(size)])  2.63 us
    pallas_call x1, Pallas kernels, shards(): pl.pallas_call(join_kernel, in_specs=[in_vmem()] * 2, out_specs=in_vmem()...  0.67 us
  transfers between devices with their start and end apart: 7, of which 6 were waited for; matrix products, arithmetic and copies ran while one was open for 0% of the time, Pallas kernels for 16%

profile of v2, /device:TPU:0, one launch (start us, length us, event | category | flops | bytes accessed | tf_op | source)
XLA Modules:
  0.0 33.1 jit_solution(7825735798199539997)
XLA Ops:
  0.6 0.0 copy-start
  0.6 5.4 %spread.1 = (bf16[64,128,256]{2,1,0:T(8,128)(2,1)S(1)}, f32[64,256]{1,0:T(8,128)S(1)}, f32[64,256]{1,0:T(8,128)S(1)}) custom-call(bf16[64,128,256]{2,1,0:T(8,128)(2,1)} %codes_hbm.1, bf16[64,256]{1,0:T(8,128)(2,1)} %signal_hbm.1, f32[128,256]{1,0:T(8,128)} %filters_ref.7), custom_call_target="tpu_custom_call" | custom-call | flops 1073741824 | bytes 4194304 | tf_op jit(solution)/shard_map/spread/pallas_call | solution.py:230
  6.0 0.5 %collective-permute-start = (f32[64,256]{1,0:T(8,128)S(1)}, f32[64,256]{1,0:T(8,128)S(1)}, u32[]{:S(2)}, u32[]{:S(2)}) collective-permute-start(f32[64,256]{1,0:T(8,128)S(1)} %get-tuple-element.15.sent_near_ref), channel_id=1, source_target_pairs={{0,1},{1,0},{2,3},{3,2},{4,5},{5,4},{6,7},{7,6},{8,9},{9,8},{10,11... | collective-permute-start | bytes 196616 | tf_op jit(solution)/shard_map/ppermute | solution.py:219
  6.6 0.7 %collective-permute-start.1 = (f32[64,256]{1,0:T(8,128)S(1)}, f32[64,256]{1,0:T(8,128)S(1)}, u32[]{:S(2)}, u32[]{:S(2)}) collective-permute-start(f32[64,256]{1,0:T(8,128)S(1)} %get-tuple-element.16.sent_far_ref), channel_id=1, source_target_pairs={{1,2},{3,4},{5,6},{7,8},{9,10},{11,12},{13,14},{2,1},{4,3},{6,5},{... | collective-permute-start | bytes 196616 | tf_op jit(solution)/shard_map/ppermute | solution.py:250
  7.2 0.2 collective-permute-done.got_near_ref
  7.5 0.0 collective-permute-done.1.got_far_ref
  7.5 2.9 %dict_grad.1 = (f32[64,256]{1,0:T(8,128)S(1)}, f32[64,256]{1,0:T(8,128)S(1)}, bf16[64,16,512]{2,1,0:T(8,128)(2,1)S(1)}) custom-call(bf16[64,128,256]{2,1,0:T(8,128)(2,1)S(1)} %get-tuple-element.14.codes_ref, f32[64,256]{1,0:T(8,128)S(1)} %get-tuple-element.15.sent_near_ref, f32[64,256]{1,0:T(8,128)S(1)} %get-tuple-element.16.sent_far_ref, ...), custom_call_target="tpu_custom_call" | custom-call | flops 1073741824 | bytes 4194304 | tf_op jit(solution)/shard_map/dict_grad/pallas_call | solution.py:252
  10.4 5.6 %collective-permute-start.2 = (f32[64,256]{1,0:T(8,128)S(1)}, f32[64,256]{1,0:T(8,128)S(1)}, u32[]{:S(2)}, u32[]{:S(2)}) collective-permute-start(f32[64,256]{1,0:T(8,128)S(1)} %get-tuple-element.18), channel_id=1, source_target_pairs={{0,1},{1,0},{2,3},{3,2},{4,5},{5,4},{6,7},{7,6},{8,9},{9,8},{10,11... | collective-permute-start | bytes 196616 | tf_op jit(solution)/shard_map/ppermute | solution.py:219
  16.1 0.9 %collective-permute-done.2 = f32[64,256]{1,0:T(8,128)S(1)} collective-permute-done((f32[64,256]{1,0:T(8,128)S(1)}, f32[64,256]{1,0:T(8,128)S(1)}, u32[]{:S(2)}, u32[]{:S(2)}) %collective-permute-start.2) | collective-permute-done | bytes 65568 | tf_op jit(solution)/shard_map/ppermute | solution.py:219
  17.0 3.1 %collective-permute-start.3 = (bf16[64,256]{1,0:T(8,128)(2,1)S(1)}, bf16[64,256]{1,0:T(8,128)(2,1)S(1)}, u32[]{:S(2)}, u32[]{:S(2)}) collective-permute-start(bf16[64,256]{1,0:T(8,128)(2,1)S(1)} %add_convert_fusion.2.sum_ref), channel_id=1, source_target_pairs={{0,2},{1,3},{2,0},{3,1},{4,6},{5,7},{6,4},{7,5},{8,10},{9,11},{10,... | collective-permute-start | bytes 98312 | tf_op jit(solution)/shard_map/ppermute | solution.py:219
  20.0 0.0 copy-done
  20.0 1.8 %codes_step.3 = (bf16[64,128,256]{2,1,0:T(8,128)(2,1)}, bf16[64,256]{1,0:T(8,128)(2,1)S(1)}) custom-call(bf16[64,256]{1,0:T(8,128)(2,1)S(1)} %add_convert_fusion.2.sum_ref, bf16[64,128,256]{2,1,0:T(8,128)(2,1)S(1)} %get-tuple-element.14.codes_ref, bf16[64,16,512]{2,1,0:T(8,128)(2,1)S(1)} %get-tuple-element.19.shifted_ref, f32[128,256]{1,0:T(8,128)S(1)} %copy-done), custom_call_target="tpu_custom_call" | custom-call | flops 352321536 | bytes 2752512 | tf_op jit(solution)/shard_map/codes_step/pallas_call | solution.py:179
  21.9 0.1 collective-permute-done.3
  22.0 2.1 %collective-permute-start.4 = (bf16[64,256]{1,0:T(8,128)(2,1)S(1)}, bf16[64,256]{1,0:T(8,128)(2,1)S(1)}, u32[]{:S(2)}, u32[]{:S(2)}) collective-permute-start(bf16[64,256]{1,0:T(8,128)(2,1)S(1)} %add_convert_fusion.1.sum_ref), channel_id=1, source_target_pairs={{0,4},{1,5},{2,6},{3,7},{4,0},{5,1},{6,2},{7,3},{8,12},{9,13},{10,... | collective-permute-start | bytes 98312 | tf_op jit(solution)/shard_map/ppermute | solution.py:219
  24.1 1.8 %codes_step.4 = (bf16[64,128,256]{2,1,0:T(8,128)(2,1)}, bf16[64,256]{1,0:T(8,128)(2,1)S(1)}) custom-call(bf16[64,256]{1,0:T(8,128)(2,1)S(1)} %add_convert_fusion.1.sum_ref, bf16[64,128,256]{2,1,0:T(8,128)(2,1)S(1)} %get-tuple-element.14.codes_ref, bf16[64,16,512]{2,1,0:T(8,128)(2,1)S(1)} %get-tuple-element.19.shifted_ref, ...), custom_call_target="tpu_custom_call", output_to_operand_aliasing={{0}: (4, {})} | custom-call | flops 352321536 | bytes 2752512 | tf_op jit(solution)/shard_map/codes_step/pallas_call | solution.py:179
  25.9 0.1 collective-permute-done.4
  26.0 3.1 %collective-permute-start.5 = (bf16[64,256]{1,0:T(8,128)(2,1)S(1)}, bf16[64,256]{1,0:T(8,128)(2,1)S(1)}, u32[]{:S(2)}, u32[]{:S(2)}) collective-permute-start(bf16[64,256]{1,0:T(8,128)(2,1)S(1)} %add_convert_fusion.sum_ref), channel_id=1, source_target_pairs={{0,8},{1,9},{2,10},{3,11},{4,12},{5,13},{6,14},{7,15},{8,0},{9,1},... | collective-permute-start | bytes 98312 | tf_op jit(solution)/shard_map/ppermute | solution.py:219
  29.1 1.8 %codes_step.5 = (bf16[64,128,256]{2,1,0:T(8,128)(2,1)}, bf16[64,256]{1,0:T(8,128)(2,1)S(1)}) custom-call(bf16[64,256]{1,0:T(8,128)(2,1)S(1)} %add_convert_fusion.sum_ref, bf16[64,128,256]{2,1,0:T(8,128)(2,1)S(1)} %get-tuple-element.14.codes_ref, bf16[64,16,512]{2,1,0:T(8,128)(2,1)S(1)} %get-tuple-element.19.shifted_ref, ...), custom_call_target="tpu_custom_call", output_to_operand_aliasing={{0}: (4, {})} | custom-call | flops 369098752 | bytes 2883584 | tf_op jit(solution)/shard_map/codes_step/pallas_call | solution.py:179
  30.9 0.1 collective-permute-done.5.last_ref
  31.0 0.1 normalize.1.mine_ref
  31.1 0.1 collective-permute-start.6
  31.2 1.2 %collective-permute-done.6.other_ref = f32[64,256]{1,0:T(8,128)S(1)} collective-permute-done((f32[64,256]{1,0:T(8,128)S(1)}, f32[64,256]{1,0:T(8,128)S(1)}, u32[]{:S(2)}, u32[]{:S(2)}) %collective-permute-start.6) | collective-permute-done | bytes 65568 | tf_op jit(solution)/shard_map/ppermute | solution.py:219
  32.4 0.7 %join.1 = f32[128,256]{1,0:T(8,128)} custom-call(f32[64,256]{1,0:T(8,128)S(1)} %normalize.1.mine_ref, f32[64,256]{1,0:T(8,128)S(1)} %collective-permute-done.6.other_ref), custom_call_target="tpu_custom_call" | custom-call | tf_op jit(solution)/shard_map/join/pallas_call | solution.py:287
  (3 shorter events, 0.0 us)
Async XLA Ops:
  0.6 19.4 %copy-start = (f32[128,256]{1,0:T(8,128)S(1)}, f32[128,256]{1,0:T(8,128)}, u32[]{:S(2)}) copy-start(f32[128,256]{1,0:T(8,128)} %filters_ref.7) | copy-start | bytes 393220
  6.0 1.4 %collective-permute-start = (f32[64,256]{1,0:T(8,128)S(1)}, f32[64,256]{1,0:T(8,128)S(1)}, u32[]{:S(2)}, u32[]{:S(2)}) collective-permute-start(f32[64,256]{1,0:T(8,128)S(1)} %get-tuple-element.15.sent_near_ref), channel_id=1, source_target_pairs={{0,1},{1,0},{2,3},{3,2},{4,5},{5,4},{6,7},{7,6},{8,9},{9,8},{10,11... | collective-permute-start | bytes 196616 | tf_op jit(solution)/shard_map/ppermute | solution.py:219
  6.6 0.9 %collective-permute-start.1 = (f32[64,256]{1,0:T(8,128)S(1)}, f32[64,256]{1,0:T(8,128)S(1)}, u32[]{:S(2)}, u32[]{:S(2)}) collective-permute-start(f32[64,256]{1,0:T(8,128)S(1)} %get-tuple-element.16.sent_far_ref), channel_id=1, source_target_pairs={{1,2},{3,4},{5,6},{7,8},{9,10},{11,12},{13,14},{2,1},{4,3},{6,5},{... | collective-permute-start | bytes 196616 | tf_op jit(solution)/shard_map/ppermute | solution.py:250
  10.4 6.5 %collective-permute-start.2 = (f32[64,256]{1,0:T(8,128)S(1)}, f32[64,256]{1,0:T(8,128)S(1)}, u32[]{:S(2)}, u32[]{:S(2)}) collective-permute-start(f32[64,256]{1,0:T(8,128)S(1)} %get-tuple-element.18), channel_id=1, source_target_pairs={{0,1},{1,0},{2,3},{3,2},{4,5},{5,4},{6,7},{7,6},{8,9},{9,8},{10,11... | collective-permute-start | bytes 196616 | tf_op jit(solution)/shard_map/ppermute | solution.py:219
  17.0 5.0 %collective-permute-start.3 = (bf16[64,256]{1,0:T(8,128)(2,1)S(1)}, bf16[64,256]{1,0:T(8,128)(2,1)S(1)}, u32[]{:S(2)}, u32[]{:S(2)}) collective-permute-start(bf16[64,256]{1,0:T(8,128)(2,1)S(1)} %add_convert_fusion.2.sum_ref), channel_id=1, source_target_pairs={{0,2},{1,3},{2,0},{3,1},{4,6},{5,7},{6,4},{7,5},{8,10},{9,11},{10,... | collective-permute-start | bytes 98312 | tf_op jit(solution)/shard_map/ppermute | solution.py:219
  22.0 4.0 %collective-permute-start.4 = (bf16[64,256]{1,0:T(8,128)(2,1)S(1)}, bf16[64,256]{1,0:T(8,128)(2,1)S(1)}, u32[]{:S(2)}, u32[]{:S(2)}) collective-permute-start(bf16[64,256]{1,0:T(8,128)(2,1)S(1)} %add_convert_fusion.1.sum_ref), channel_id=1, source_target_pairs={{0,4},{1,5},{2,6},{3,7},{4,0},{5,1},{6,2},{7,3},{8,12},{9,13},{10,... | collective-permute-start | bytes 98312 | tf_op jit(solution)/shard_map/ppermute | solution.py:219
  26.0 5.0 %collective-permute-start.5 = (bf16[64,256]{1,0:T(8,128)(2,1)S(1)}, bf16[64,256]{1,0:T(8,128)(2,1)S(1)}, u32[]{:S(2)}, u32[]{:S(2)}) collective-permute-start(bf16[64,256]{1,0:T(8,128)(2,1)S(1)} %add_convert_fusion.sum_ref), channel_id=1, source_target_pairs={{0,8},{1,9},{2,10},{3,11},{4,12},{5,13},{6,14},{7,15},{8,0},{9,1},... | collective-permute-start | bytes 98312 | tf_op jit(solution)/shard_map/ppermute | solution.py:219
  31.1 1.3 %collective-permute-start.6 = (f32[64,256]{1,0:T(8,128)S(1)}, f32[64,256]{1,0:T(8,128)S(1)}, u32[]{:S(2)}, u32[]{:S(2)}) collective-permute-start(f32[64,256]{1,0:T(8,128)S(1)} %normalize.1.mine_ref), channel_id=1, source_target_pairs={{0,1},{1,0},{2,3},{3,2},{4,5},{5,4},{6,7},{7,6},{8,9},{9,8},{10,11... | collective-permute-start | bytes 196616 | tf_op jit(solution)/shard_map/ppermute | solution.py:219

commit v3 on v2

--- a/solution.py
+++ b/solution.py
@@ -214,6 +214,20 @@
     out_ref[half:, :] = jnp.where(even, other_ref[...], mine_ref[...])
 
 
+def exchange_rounds(devices):
+    distance, rounds = 2, []
+    while distance < devices:
+        both = 4 * distance < devices
+        rounds.append([distance, 2 * distance, 3 * distance] if both else [distance])
+        distance *= 4 if both else 2
+    return rounds
+
+
+def part_ends(chans, rounds):
+    weights = [4 if len(distances) > 1 else 3 for distances in rounds]
+    return [chans * sum(weights[:n]) // sum(weights) for n in range(len(rounds) + 1)]
+
+
 def exchange(block, distance):
     size = lax.axis_size("tm")
     return lax.ppermute(block, "tm", [(i, i ^ distance) for i in range(size)])
@@ -246,8 +260,8 @@
 
     across = [(i, i + 1) for i in range(1, devices - 1, 2)]
     across += [(j, i) for i, j in across]
+    got_far = lax.ppermute(sent_far, "tm", across)
     got_near = exchange(sent_near, 1)
-    got_far = lax.ppermute(sent_far, "tm", across)
 
     mine, other, shifted = pl.pallas_call(
         dict_kernel,
@@ -265,17 +279,18 @@
     )(held, sent_near, sent_far, got_near, got_far)
 
     total = mine + exchange(other, 1)
-    distances = [2]
-    while 2 * distances[-1] < devices:
-        distances.append(2 * distances[-1])
-    new_codes, first = None, 0
-    for place, distance in enumerate(distances):
+    rounds = exchange_rounds(devices)
+    ends = part_ends(chans, rounds)
+    new_codes = None
+    for place, distances in enumerate(rounds):
         sent = total.astype(HOP)
-        received = exchange(sent, distance)
-        end = chans * (place + 1) // len(distances)
+        received = [exchange(sent, d) for d in distances]
+        first, end = ends[place], ends[place + 1]
         new_codes, kept = step_codes(first, end - first, sent, held, shifted, filters, new_codes)
-        first = end
-        total = kept.astype(F32) + received.astype(F32)
+        if place + 1 < len(rounds):
+            total = kept.astype(F32) + received[0].astype(F32)
+            if len(received) > 1:
+                total += received[1].astype(F32) + received[2].astype(F32)
     mine = pl.pallas_call(
         functools.partial(normalize_kernel, float(chans * local_len * devices)),
         in_specs=[in_vmem()] * 3,
@@ -283,7 +298,7 @@
         out_shape=jax.ShapeDtypeStruct((half, taps), F32),
         compiler_params=params,
         name="normalize",
-    )(kept, received, filters)
+    )(kept, received[0], filters)
     new_filters = pl.pallas_call(
         join_kernel,
         in_specs=[in_vmem()] * 2,

time: 33.2 us -> 32.6 us (0.982)
  waiting for transfers between devices: 2.63 us -> 3.64 us
  starting transfers between devices: 15.2 us -> 14.3 us
  Pallas kernels: 14.5 us -> 13.8 us
    ppermute x6 -> x7, waiting for transfers between devices: 2.63 us -> 3.64 us  [exchange(): return lax.ppermute(block, 'tm', [(i, i ^ distance) for i in range(size)])]
    ppermute x6 -> x7, starting transfers between devices: 14.5 us -> 13.6 us  [exchange(): return lax.ppermute(block, 'tm', [(i, i ^ distance) for i in range(size)])]
    pallas_call x3 -> x2, Pallas kernels: 5.42 us -> 4.65 us  [step_codes(): pl.pallas_call(functools.partial(codes_kernel, first), in_specs=[in_vmem(...]
  transfers between devices with their start and end apart: 7 -> 8, of which waited for: 6 -> 6; matrix products, arithmetic and copies ran while one was open for 0% -> 0% of each run, Pallas kernels for 16% -> 14%
where the time goes in v3:
time: 32.6 us; the launch traced here: 32.4 us
  starting transfers between devices  14.3 us (44%)
  Pallas kernels  13.8 us (42%)
  waiting for transfers between devices  3.64 us (11%)
  between operations  0.71 us (2%)
    ppermute x7, starting transfers between devices, exchange(): return lax.ppermute(block, 'tm', [(i, i ^ distance) for i in range(size)])  13.6 us
    pallas_call x1, Pallas kernels, shards(): pl.pallas_call(spread_kernel, in_specs=[in_hbm()] * 3, out_specs=[in_vmem...  5.38 us
    pallas_call x2, Pallas kernels, step_codes(): pl.pallas_call(functools.partial(codes_kernel, first), in_specs=[in_vmem(...  4.65 us
    ppermute x7, waiting for transfers between devices, exchange(): return lax.ppermute(block, 'tm', [(i, i ^ distance) for i in range(size)])  3.64 us
    pallas_call x1, Pallas kernels, shards(): pl.pallas_call(dict_kernel, in_specs=[in_vmem()] * 5, out_specs=[in_vmem(...  2.95 us
    pallas_call x1, Pallas kernels, shards(): pl.pallas_call(join_kernel, in_specs=[in_vmem()] * 2, out_specs=in_vmem()...  0.67 us
    ppermute x1, starting transfers between devices, shards(): got_far = lax.ppermute(sent_far, 'tm', across)  0.65 us
  transfers between devices with their start and end apart: 8, of which 6 were waited for; matrix products, arithmetic and copies ran while one was open for 0% of the time, Pallas kernels for 14%

profile of v3, /device:TPU:0, one launch (start us, length us, event | category | flops | bytes accessed | tf_op | source)
XLA Modules:
  0.0 32.4 jit_solution(9615724872507477759)
XLA Ops:
  0.6 0.0 copy-start
  0.6 5.4 %spread.1 = (bf16[64,128,256]{2,1,0:T(8,128)(2,1)S(1)}, f32[64,256]{1,0:T(8,128)S(1)}, f32[64,256]{1,0:T(8,128)S(1)}) custom-call(bf16[64,128,256]{2,1,0:T(8,128)(2,1)} %codes_hbm.1, bf16[64,256]{1,0:T(8,128)(2,1)} %signal_hbm.1, f32[128,256]{1,0:T(8,128)} %filters_ref.5), custom_call_target="tpu_custom_call" | custom-call | flops 1073741824 | bytes 4194304 | tf_op jit(solution)/shard_map/spread/pallas_call | solution.py:244
  6.0 0.5 %collective-permute-start = (f32[64,256]{1,0:T(8,128)S(1)}, f32[64,256]{1,0:T(8,128)S(1)}, u32[]{:S(2)}, u32[]{:S(2)}) collective-permute-start(f32[64,256]{1,0:T(8,128)S(1)} %get-tuple-element.13.sent_near_ref), channel_id=1, source_target_pairs={{0,1},{1,0},{2,3},{3,2},{4,5},{5,4},{6,7},{7,6},{8,9},{9,8},{10,11... | collective-permute-start | bytes 196616 | tf_op jit(solution)/shard_map/ppermute | solution.py:233
  6.6 0.7 %collective-permute-start.1 = (f32[64,256]{1,0:T(8,128)S(1)}, f32[64,256]{1,0:T(8,128)S(1)}, u32[]{:S(2)}, u32[]{:S(2)}) collective-permute-start(f32[64,256]{1,0:T(8,128)S(1)} %get-tuple-element.14.sent_far_ref), channel_id=1, source_target_pairs={{1,2},{3,4},{5,6},{7,8},{9,10},{11,12},{13,14},{2,1},{4,3},{6,5},{... | collective-permute-start | bytes 196616 | tf_op jit(solution)/shard_map/ppermute | solution.py:263
  7.2 0.2 collective-permute-done.got_near_ref
  7.5 0.0 collective-permute-done.1.got_far_ref
  7.5 2.9 %dict_grad.1 = (f32[64,256]{1,0:T(8,128)S(1)}, f32[64,256]{1,0:T(8,128)S(1)}, bf16[64,16,512]{2,1,0:T(8,128)(2,1)S(1)}) custom-call(bf16[64,128,256]{2,1,0:T(8,128)(2,1)S(1)} %get-tuple-element.12.codes_ref, f32[64,256]{1,0:T(8,128)S(1)} %get-tuple-element.13.sent_near_ref, f32[64,256]{1,0:T(8,128)S(1)} %get-tuple-element.14.sent_far_ref, ...), custom_call_target="tpu_custom_call" | custom-call | flops 1073741824 | bytes 4194304 | tf_op jit(solution)/shard_map/dict_grad/pallas_call | solution.py:266
  10.4 5.6 %collective-permute-start.2 = (f32[64,256]{1,0:T(8,128)S(1)}, f32[64,256]{1,0:T(8,128)S(1)}, u32[]{:S(2)}, u32[]{:S(2)}) collective-permute-start(f32[64,256]{1,0:T(8,128)S(1)} %get-tuple-element.16), channel_id=1, source_target_pairs={{0,1},{1,0},{2,3},{3,2},{4,5},{5,4},{6,7},{7,6},{8,9},{9,8},{10,11... | collective-permute-start | bytes 196616 | tf_op jit(solution)/shard_map/ppermute | solution.py:233
  16.1 0.9 %collective-permute-done.2 = f32[64,256]{1,0:T(8,128)S(1)} collective-permute-done((f32[64,256]{1,0:T(8,128)S(1)}, f32[64,256]{1,0:T(8,128)S(1)}, u32[]{:S(2)}, u32[]{:S(2)}) %collective-permute-start.2) | collective-permute-done | bytes 65568 | tf_op jit(solution)/shard_map/ppermute | solution.py:233
  17.0 4.1 %collective-permute-start.5 = (bf16[64,256]{1,0:T(8,128)(2,1)S(1)}, bf16[64,256]{1,0:T(8,128)(2,1)S(1)}, u32[]{:S(2)}, u32[]{:S(2)}) collective-permute-start(bf16[64,256]{1,0:T(8,128)(2,1)S(1)} %add_convert_fusion.1.sum_ref), channel_id=1, source_target_pairs={{0,6},{1,7},{2,4},{3,5},{4,2},{5,3},{6,0},{7,1},{8,14},{9,15},{10,... | collective-permute-start | bytes 98312 | tf_op jit(solution)/shard_map/ppermute | solution.py:233
  21.1 0.4 %collective-permute-start.4 = (bf16[64,256]{1,0:T(8,128)(2,1)S(1)}, bf16[64,256]{1,0:T(8,128)(2,1)S(1)}, u32[]{:S(2)}, u32[]{:S(2)}) collective-permute-start(bf16[64,256]{1,0:T(8,128)(2,1)S(1)} %add_convert_fusion.1.sum_ref), channel_id=1, source_target_pairs={{0,4},{1,5},{2,6},{3,7},{4,0},{5,1},{6,2},{7,3},{8,12},{9,13},{10,... | collective-permute-start | bytes 98312 | tf_op jit(solution)/shard_map/ppermute | solution.py:233
  21.5 0.2 collective-permute-start.3
  21.7 0.0 copy-done
  21.7 2.5 %codes_step.2 = (bf16[64,128,256]{2,1,0:T(8,128)(2,1)}, bf16[64,256]{1,0:T(8,128)(2,1)S(1)}) custom-call(bf16[64,256]{1,0:T(8,128)(2,1)S(1)} %add_convert_fusion.1.sum_ref, bf16[64,128,256]{2,1,0:T(8,128)(2,1)S(1)} %get-tuple-element.12.codes_ref, bf16[64,16,512]{2,1,0:T(8,128)(2,1)S(1)} %get-tuple-element.17.shifted_ref, f32[128,256]{1,0:T(8,128)S(1)} %copy-done), custom_call_target="tpu_custom_call" | custom-call | flops 603979776 | bytes 4718592 | tf_op jit(solution)/shard_map/codes_step/pallas_call | solution.py:179
  24.2 0.0 collective-permute-done.5
  24.2 0.8 %collective-permute-done.4 = bf16[64,256]{1,0:T(8,128)(2,1)S(1)} collective-permute-done((bf16[64,256]{1,0:T(8,128)(2,1)S(1)}, bf16[64,256]{1,0:T(8,128)(2,1)S(1)}, u32[]{:S(2)}, u32[]{:S(2)}) %collective-permute-start.4) | collective-permute-done | bytes 32800 | tf_op jit(solution)/shard_map/ppermute | solution.py:233
  25.0 0.4 %collective-permute-done.3 = bf16[64,256]{1,0:T(8,128)(2,1)S(1)} collective-permute-done((bf16[64,256]{1,0:T(8,128)(2,1)S(1)}, bf16[64,256]{1,0:T(8,128)(2,1)S(1)}, u32[]{:S(2)}, u32[]{:S(2)}) %collective-permute-start.3) | collective-permute-done | bytes 32800 | tf_op jit(solution)/shard_map/ppermute | solution.py:233
  25.4 2.7 %collective-permute-start.6 = (bf16[64,256]{1,0:T(8,128)(2,1)S(1)}, bf16[64,256]{1,0:T(8,128)(2,1)S(1)}, u32[]{:S(2)}, u32[]{:S(2)}) collective-permute-start(bf16[64,256]{1,0:T(8,128)(2,1)S(1)} %add_convert_fusion.sum_ref), channel_id=1, source_target_pairs={{0,8},{1,9},{2,10},{3,11},{4,12},{5,13},{6,14},{7,15},{8,0},{9,1},... | collective-permute-start | bytes 98312 | tf_op jit(solution)/shard_map/ppermute | solution.py:233
  28.1 2.2 %codes_step.3 = (bf16[64,128,256]{2,1,0:T(8,128)(2,1)}, bf16[64,256]{1,0:T(8,128)(2,1)S(1)}) custom-call(bf16[64,256]{1,0:T(8,128)(2,1)S(1)} %add_convert_fusion.sum_ref, bf16[64,128,256]{2,1,0:T(8,128)(2,1)S(1)} %get-tuple-element.12.codes_ref, bf16[64,16,512]{2,1,0:T(8,128)(2,1)S(1)} %get-tuple-element.17.shifted_ref, ...), custom_call_target="tpu_custom_call", output_to_operand_aliasing={{0}: (4, {})} | custom-call | flops 469762048 | bytes 3670016 | tf_op jit(solution)/shard_map/codes_step/pallas_call | solution.py:179
  30.3 0.1 collective-permute-done.6.last_ref
  30.3 0.1 normalize.1.mine_ref
  30.4 0.1 collective-permute-start.7
  30.5 1.2 %collective-permute-done.7.other_ref = f32[64,256]{1,0:T(8,128)S(1)} collective-permute-done((f32[64,256]{1,0:T(8,128)S(1)}, f32[64,256]{1,0:T(8,128)S(1)}, u32[]{:S(2)}, u32[]{:S(2)}) %collective-permute-start.7) | collective-permute-done | bytes 65568 | tf_op jit(solution)/shard_map/ppermute | solution.py:233
  31.8 0.7 %join.1 = f32[128,256]{1,0:T(8,128)} custom-call(f32[64,256]{1,0:T(8,128)S(1)} %normalize.1.mine_ref, f32[64,256]{1,0:T(8,128)S(1)} %collective-permute-done.7.other_ref), custom_call_target="tpu_custom_call" | custom-call | tf_op jit(solution)/shard_map/join/pallas_call | solution.py:302
  (2 shorter events, 0.0 us)
Async XLA Ops:
  0.6 21.1 %copy-start = (f32[128,256]{1,0:T(8,128)S(1)}, f32[128,256]{1,0:T(8,128)}, u32[]{:S(2)}) copy-start(f32[128,256]{1,0:T(8,128)} %filters_ref.5) | copy-start | bytes 393220
  6.0 1.4 %collective-permute-start = (f32[64,256]{1,0:T(8,128)S(1)}, f32[64,256]{1,0:T(8,128)S(1)}, u32[]{:S(2)}, u32[]{:S(2)}) collective-permute-start(f32[64,256]{1,0:T(8,128)S(1)} %get-tuple-element.13.sent_near_ref), channel_id=1, source_target_pairs={{0,1},{1,0},{2,3},{3,2},{4,5},{5,4},{6,7},{7,6},{8,9},{9,8},{10,11... | collective-permute-start | bytes 196616 | tf_op jit(solution)/shard_map/ppermute | solution.py:233
  6.6 0.9 %collective-permute-start.1 = (f32[64,256]{1,0:T(8,128)S(1)}, f32[64,256]{1,0:T(8,128)S(1)}, u32[]{:S(2)}, u32[]{:S(2)}) collective-permute-start(f32[64,256]{1,0:T(8,128)S(1)} %get-tuple-element.14.sent_far_ref), channel_id=1, source_target_pairs={{1,2},{3,4},{5,6},{7,8},{9,10},{11,12},{13,14},{2,1},{4,3},{6,5},{... | collective-permute-start | bytes 196616 | tf_op jit(solution)/shard_map/ppermute | solution.py:263
  10.4 6.5 %collective-permute-start.2 = (f32[64,256]{1,0:T(8,128)S(1)}, f32[64,256]{1,0:T(8,128)S(1)}, u32[]{:S(2)}, u32[]{:S(2)}) collective-permute-start(f32[64,256]{1,0:T(8,128)S(1)} %get-tuple-element.16), channel_id=1, source_target_pairs={{0,1},{1,0},{2,3},{3,2},{4,5},{5,4},{6,7},{7,6},{8,9},{9,8},{10,11... | collective-permute-start | bytes 196616 | tf_op jit(solution)/shard_map/ppermute | solution.py:233
  17.0 7.2 %collective-permute-start.5 = (bf16[64,256]{1,0:T(8,128)(2,1)S(1)}, bf16[64,256]{1,0:T(8,128)(2,1)S(1)}, u32[]{:S(2)}, u32[]{:S(2)}) collective-permute-start(bf16[64,256]{1,0:T(8,128)(2,1)S(1)} %add_convert_fusion.1.sum_ref), channel_id=1, source_target_pairs={{0,6},{1,7},{2,4},{3,5},{4,2},{5,3},{6,0},{7,1},{8,14},{9,15},{10,... | collective-permute-start | bytes 98312 | tf_op jit(solution)/shard_map/ppermute | solution.py:233
  21.1 3.9 %collective-permute-start.4 = (bf16[64,256]{1,0:T(8,128)(2,1)S(1)}, bf16[64,256]{1,0:T(8,128)(2,1)S(1)}, u32[]{:S(2)}, u32[]{:S(2)}) collective-permute-start(bf16[64,256]{1,0:T(8,128)(2,1)S(1)} %add_convert_fusion.1.sum_ref), channel_id=1, source_target_pairs={{0,4},{1,5},{2,6},{3,7},{4,0},{5,1},{6,2},{7,3},{8,12},{9,13},{10,... | collective-permute-start | bytes 98312 | tf_op jit(solution)/shard_map/ppermute | solution.py:233
  21.5 3.9 %collective-permute-start.3 = (bf16[64,256]{1,0:T(8,128)(2,1)S(1)}, bf16[64,256]{1,0:T(8,128)(2,1)S(1)}, u32[]{:S(2)}, u32[]{:S(2)}) collective-permute-start(bf16[64,256]{1,0:T(8,128)(2,1)S(1)} %add_convert_fusion.1.sum_ref), channel_id=1, source_target_pairs={{0,2},{1,3},{2,0},{3,1},{4,6},{5,7},{6,4},{7,5},{8,10},{9,11},{10,... | collective-permute-start | bytes 98312 | tf_op jit(solution)/shard_map/ppermute | solution.py:233
  25.4 4.9 %collective-permute-start.6 = (bf16[64,256]{1,0:T(8,128)(2,1)S(1)}, bf16[64,256]{1,0:T(8,128)(2,1)S(1)}, u32[]{:S(2)}, u32[]{:S(2)}) collective-permute-start(bf16[64,256]{1,0:T(8,128)(2,1)S(1)} %add_convert_fusion.sum_ref), channel_id=1, source_target_pairs={{0,8},{1,9},{2,10},{3,11},{4,12},{5,13},{6,14},{7,15},{8,0},{9,1},... | collective-permute-start | bytes 98312 | tf_op jit(solution)/shard_map/ppermute | solution.py:233
  30.4 1.3 %collective-permute-start.7 = (f32[64,256]{1,0:T(8,128)S(1)}, f32[64,256]{1,0:T(8,128)S(1)}, u32[]{:S(2)}, u32[]{:S(2)}) collective-permute-start(f32[64,256]{1,0:T(8,128)S(1)} %normalize.1.mine_ref), channel_id=1, source_target_pairs={{0,1},{1,0},{2,3},{3,2},{4,5},{5,4},{6,7},{7,6},{8,9},{9,8},{10,11... | collective-permute-start | bytes 196616 | tf_op jit(solution)/shard_map/ppermute | solution.py:233

commit v4 on v3

--- a/solution.py
+++ b/solution.py
@@ -51,7 +51,7 @@
     return pl.BlockSpec(memory_space=pltpu.HBM)
 
 
-def spread_kernel(codes_hbm, signal_hbm, filters_hbm, codes_ref, near_ref, far_ref, signal_ref, filters_ref, shear_ref, arrived, small):
+def spread_kernel(codes_hbm, signal_hbm, filters_hbm, codes_ref, filters_ref, far_ref, far_sent_ref, near_ref, signal_ref, shear_ref, arrived, small):
     chans, count, local_len = codes_ref.shape
     taps = filters_ref.shape[1]
     filters_in = pltpu.make_async_copy(filters_hbm, filters_ref, small.at[0])
@@ -104,7 +104,9 @@
     onward = total[:, taps:]
     even = parity() == 0
     near_ref[...] = jnp.where(even, onward, own)
-    far_ref[...] = jnp.where(even, own, onward)
+    far = jnp.where(even, own, onward)
+    far_ref[...] = far
+    far_sent_ref[...] = far.astype(far_sent_ref.dtype)
 
 
 def hankel_block(shifted, lane):
@@ -129,23 +131,25 @@
     last = me == lax.axis_size("tm") - 1
     own = jnp.where(even, sent_far_ref[...], sent_near_ref[...])
     onward = jnp.where(even, sent_near_ref[...], sent_far_ref[...])
-    before = jnp.where(even, got_far_ref[...], got_near_ref[...])
-    after = jnp.where(even, got_near_ref[...], got_far_ref[...])
+    got_far = got_far_ref[...].astype(F32)
+    before = jnp.where(even, got_far, got_near_ref[...])
+    after = jnp.where(even, got_near_ref[...], got_far)
     following = jnp.where(last, 0.0, onward + after)
-    error = jnp.concatenate([own + before, following], axis=1).astype(BF16).astype(F32)
+    error = jnp.concatenate([own + before, following], axis=1).astype(BF16)
     width = error.shape[1]
-    for r in range(PACK):
-        moved = pltpu.roll(error, width - r, 1) if r else error
-        for n in range(4):
-            wide_ref[n, pl.ds(r, chans, stride=PACK), :] = moved[:, n * LANES : (n + 1) * LANES]
     lane = lane_index((PACK, LANES))
-
-    total = jnp.zeros((count, error.shape[1] // 2), F32)
-    for c in range(chans):
-        rows = pl.ds(c * PACK, PACK)
-        shifted = jnp.concatenate([wide_ref[n, rows, :] for n in range(4)], axis=1).astype(BF16)
-        shifted_ref[c] = shifted
-        total += jnp.dot(codes_ref[c], hankel_block(shifted, lane), preferred_element_type=F32)
+    total = jnp.zeros((count, width // 2), F32)
+    for first in range(0, chans, PACK):
+        rows = error[first : first + PACK]
+        for r in range(PACK):
+            moved = (pltpu.roll(rows, width - r, 1) if r else rows).astype(F32)
+            for n in range(4):
+                wide_ref[n, pl.ds(first * PACK + r, PACK, stride=PACK), :] = moved[:, n * LANES : (n + 1) * LANES]
+        for c in range(first, first + PACK):
+            rows_c = pl.ds(c * PACK, PACK)
+            shifted = jnp.concatenate([wide_ref[n, rows_c, :] for n in range(4)], axis=1).astype(BF16)
+            shifted_ref[c] = shifted
+            total += jnp.dot(codes_ref[c], hankel_block(shifted, lane), preferred_element_type=F32)
     half = count // 2
     mine_ref[...] = jnp.where(even, total[:half], total[half:])
     other_ref[...] = jnp.where(even, total[half:], total[:half])
@@ -241,14 +245,19 @@
     params = pltpu.CompilerParams(vmem_limit_bytes=VMEM_BYTES)
     halo = jax.ShapeDtypeStruct((chans, taps), F32)
     matmul_flops = 2 * chans * count * local_len * taps
-    held, sent_near, sent_far = pl.pallas_call(
+    held, held_filters, far, sent_far, sent_near = pl.pallas_call(
         spread_kernel,
         in_specs=[in_hbm()] * 3,
-        out_specs=[in_vmem()] * 3,
-        out_shape=[jax.ShapeDtypeStruct(codes.shape, BF16), halo, halo],
+        out_specs=[in_vmem()] * 5,
+        out_shape=[
+            jax.ShapeDtypeStruct(codes.shape, BF16),
+            jax.ShapeDtypeStruct(filters.shape, F32),
+            halo,
+            jax.ShapeDtypeStruct(halo.shape, HOP),
+            halo,
+        ],
         scratch_shapes=[
             pltpu.VMEM(signal.shape, BF16),
-            pltpu.VMEM(filters.shape, F32),
             pltpu.VMEM((4, 8 * chans, LANES), F32),
             pltpu.SemaphoreType.DMA((CHUNKS,)),
             pltpu.SemaphoreType.DMA((2,)),
@@ -276,7 +285,7 @@
         compiler_params=params,
         cost_estimate=pl.CostEstimate(flops=matmul_flops, bytes_accessed=codes.size * 2, transcendentals=0),
         name="dict_grad",
-    )(held, sent_near, sent_far, got_near, got_far)
+    )(held, sent_near, far, got_near, got_far)
 
     total = mine + exchange(other, 1)
     rounds = exchange_rounds(devices)
@@ -286,7 +295,7 @@
         sent = total.astype(HOP)
         received = [exchange(sent, d) for d in distances]
         first, end = ends[place], ends[place + 1]
-        new_codes, kept = step_codes(first, end - first, sent, held, shifted, filters, new_codes)
+        new_codes, kept = step_codes(first, end - first, sent, held, shifted, held_filters, new_codes)
         if place + 1 < len(rounds):
             total = kept.astype(F32) + received[0].astype(F32)
             if len(received) > 1:
@@ -298,7 +307,7 @@
         out_shape=jax.ShapeDtypeStruct((half, taps), F32),
         compiler_params=params,
         name="normalize",
-    )(kept, received[0], filters)
+    )(kept, received[0], held_filters)
     new_filters = pl.pallas_call(
         join_kernel,
         in_specs=[in_vmem()] * 2,

time: 32.6 us -> 32.1 us (0.985)
  starting transfers between devices: 14.3 us -> 13.9 us
    ppermute x7, starting transfers between devices: 13.6 us -> 13.3 us  [exchange(): return lax.ppermute(block, 'tm', [(i, i ^ distance) for i in range(size)])]
  transfers between devices with their start and end apart: 8 -> 8, of which waited for: 6 -> 6; matrix products, arithmetic and copies ran while one was open for 0% -> 0% of each run, Pallas kernels for 14% -> 15%
where the time goes in v4:
time: 32.1 us; the launch traced here: 32 us
  starting transfers between devices  13.9 us (43%)
  Pallas kernels  13.7 us (43%)
  waiting for transfers between devices  3.66 us (11%)
  between operations  0.71 us (2%)
    ppermute x7, starting transfers between devices, exchange(): return lax.ppermute(block, 'tm', [(i, i ^ distance) for i in range(size)])  13.3 us
    pallas_call x1, Pallas kernels, shards(): pl.pallas_call(spread_kernel, in_specs=[in_hbm()] * 3, out_specs=[in_vmem...  5.36 us
    pallas_call x2, Pallas kernels, step_codes(): pl.pallas_call(functools.partial(codes_kernel, first), in_specs=[in_vmem(...  4.64 us
    ppermute x7, waiting for transfers between devices, exchange(): return lax.ppermute(block, 'tm', [(i, i ^ distance) for i in range(size)])  3.66 us
    pallas_call x1, Pallas kernels, shards(): pl.pallas_call(dict_kernel, in_specs=[in_vmem()] * 5, out_specs=[in_vmem(...  2.87 us
    pallas_call x1, Pallas kernels, shards(): pl.pallas_call(join_kernel, in_specs=[in_vmem()] * 2, out_specs=in_vmem()...  0.67 us
    ppermute x1, starting transfers between devices, shards(): got_far = lax.ppermute(sent_far, 'tm', across)  0.65 us
  transfers between devices with their start and end apart: 8, of which 6 were waited for; matrix products, arithmetic and copies ran while one was open for 0% of the time, Pallas kernels for 15%

profile of v4, /device:TPU:0, one launch (start us, length us, event | category | flops | bytes accessed | tf_op | source)
XLA Modules:
  0.0 32.0 jit_solution(16963038309073166096)
XLA Ops:
  0.6 5.4 %spread.1 = (bf16[64,128,256]{2,1,0:T(8,128)(2,1)S(1)}, f32[128,256]{1,0:T(8,128)S(1)}, f32[64,256]{1,0:T(8,128)S(1)}, bf16[64,256]{1,0:T(8,128)(2,1)S(1)}, f32[64,256]{1,0:T(8,128)S(1)}) custom-call(bf16[64,128,256]{2,1,0:T(8,128)(2,1)} %codes_hbm.1, bf16[64,256]{1,0:T(8,128)(2,1)} %signal_hbm.1, f32[128,256]{1,0:T(8,128)} %filters_hbm.1), custom_call_target="tpu_custom_call" | custom-call | flops 1073741824 | bytes 4194304 | tf_op jit(solution)/shard_map/spread/pallas_call | solution.py:248
  6.0 0.5 %collective-permute-start = (f32[64,256]{1,0:T(8,128)S(1)}, f32[64,256]{1,0:T(8,128)S(1)}, u32[]{:S(2)}, u32[]{:S(2)}) collective-permute-start(f32[64,256]{1,0:T(8,128)S(1)} %get-tuple-element.15.sent_near_ref), channel_id=1, source_target_pairs={{0,1},{1,0},{2,3},{3,2},{4,5},{5,4},{6,7},{7,6},{8,9},{9,8},{10,11... | collective-permute-start | bytes 196616 | tf_op jit(solution)/shard_map/ppermute | solution.py:237
  6.5 0.7 %collective-permute-start.1 = (bf16[64,256]{1,0:T(8,128)(2,1)S(1)}, bf16[64,256]{1,0:T(8,128)(2,1)S(1)}, u32[]{:S(2)}, u32[]{:S(2)}) collective-permute-start(bf16[64,256]{1,0:T(8,128)(2,1)S(1)} %get-tuple-element.17), channel_id=1, source_target_pairs={{1,2},{3,4},{5,6},{7,8},{9,10},{11,12},{13,14},{2,1},{4,3},{6,5},{... | collective-permute-start | bytes 98312 | tf_op jit(solution)/shard_map/ppermute | solution.py:272
  7.2 0.0 collective-permute-done.1.got_far_ref
  7.2 0.2 collective-permute-done.got_near_ref
  7.4 2.9 %dict_grad.1 = (f32[64,256]{1,0:T(8,128)S(1)}, f32[64,256]{1,0:T(8,128)S(1)}, bf16[64,16,512]{2,1,0:T(8,128)(2,1)S(1)}) custom-call(bf16[64,128,256]{2,1,0:T(8,128)(2,1)S(1)} %get-tuple-element.14.codes_ref, f32[64,256]{1,0:T(8,128)S(1)} %get-tuple-element.15.sent_near_ref, f32[64,256]{1,0:T(8,128)S(1)} %get-tuple-element.16.sent_far_ref, ...), custom_call_target="tpu_custom_call" | custom-call | flops 1073741824 | bytes 4194304 | tf_op jit(solution)/shard_map/dict_grad/pallas_call | solution.py:275
  10.3 5.3 %collective-permute-start.2 = (f32[64,256]{1,0:T(8,128)S(1)}, f32[64,256]{1,0:T(8,128)S(1)}, u32[]{:S(2)}, u32[]{:S(2)}) collective-permute-start(f32[64,256]{1,0:T(8,128)S(1)} %get-tuple-element.19), channel_id=1, source_target_pairs={{0,1},{1,0},{2,3},{3,2},{4,5},{5,4},{6,7},{7,6},{8,9},{9,8},{10,11... | collective-permute-start | bytes 196616 | tf_op jit(solution)/shard_map/ppermute | solution.py:237
  15.6 0.9 %collective-permute-done.2 = f32[64,256]{1,0:T(8,128)S(1)} collective-permute-done((f32[64,256]{1,0:T(8,128)S(1)}, f32[64,256]{1,0:T(8,128)S(1)}, u32[]{:S(2)}, u32[]{:S(2)}) %collective-permute-start.2) | collective-permute-done | bytes 65568 | tf_op jit(solution)/shard_map/ppermute | solution.py:237
  16.5 4.1 %collective-permute-start.5 = (bf16[64,256]{1,0:T(8,128)(2,1)S(1)}, bf16[64,256]{1,0:T(8,128)(2,1)S(1)}, u32[]{:S(2)}, u32[]{:S(2)}) collective-permute-start(bf16[64,256]{1,0:T(8,128)(2,1)S(1)} %add_convert_fusion.1.sum_ref), channel_id=1, source_target_pairs={{0,6},{1,7},{2,4},{3,5},{4,2},{5,3},{6,0},{7,1},{8,14},{9,15},{10,... | collective-permute-start | bytes 98312 | tf_op jit(solution)/shard_map/ppermute | solution.py:237
  20.6 0.4 %collective-permute-start.4 = (bf16[64,256]{1,0:T(8,128)(2,1)S(1)}, bf16[64,256]{1,0:T(8,128)(2,1)S(1)}, u32[]{:S(2)}, u32[]{:S(2)}) collective-permute-start(bf16[64,256]{1,0:T(8,128)(2,1)S(1)} %add_convert_fusion.1.sum_ref), channel_id=1, source_target_pairs={{0,4},{1,5},{2,6},{3,7},{4,0},{5,1},{6,2},{7,3},{8,12},{9,13},{10,... | collective-permute-start | bytes 98312 | tf_op jit(solution)/shard_map/ppermute | solution.py:237
  21.1 0.2 collective-permute-start.3
  21.3 2.5 %codes_step.2 = (bf16[64,128,256]{2,1,0:T(8,128)(2,1)}, bf16[64,256]{1,0:T(8,128)(2,1)S(1)}) custom-call(bf16[64,256]{1,0:T(8,128)(2,1)S(1)} %add_convert_fusion.1.sum_ref, bf16[64,128,256]{2,1,0:T(8,128)(2,1)S(1)} %get-tuple-element.14.codes_ref, bf16[64,16,512]{2,1,0:T(8,128)(2,1)S(1)} %get-tuple-element.20.shifted_ref, ...), custom_call_target="tpu_custom_call" | custom-call | flops 603979776 | bytes 4718592 | tf_op jit(solution)/shard_map/codes_step/pallas_call | solution.py:183
  23.8 0.0 collective-permute-done.5
  23.8 0.8 %collective-permute-done.4 = bf16[64,256]{1,0:T(8,128)(2,1)S(1)} collective-permute-done((bf16[64,256]{1,0:T(8,128)(2,1)S(1)}, bf16[64,256]{1,0:T(8,128)(2,1)S(1)}, u32[]{:S(2)}, u32[]{:S(2)}) %collective-permute-start.4) | collective-permute-done | bytes 32800 | tf_op jit(solution)/shard_map/ppermute | solution.py:237
  24.5 0.4 %collective-permute-done.3 = bf16[64,256]{1,0:T(8,128)(2,1)S(1)} collective-permute-done((bf16[64,256]{1,0:T(8,128)(2,1)S(1)}, bf16[64,256]{1,0:T(8,128)(2,1)S(1)}, u32[]{:S(2)}, u32[]{:S(2)}) %collective-permute-start.3) | collective-permute-done | bytes 32800 | tf_op jit(solution)/shard_map/ppermute | solution.py:237
  25.0 2.6 %collective-permute-start.6 = (bf16[64,256]{1,0:T(8,128)(2,1)S(1)}, bf16[64,256]{1,0:T(8,128)(2,1)S(1)}, u32[]{:S(2)}, u32[]{:S(2)}) collective-permute-start(bf16[64,256]{1,0:T(8,128)(2,1)S(1)} %add_convert_fusion.sum_ref), channel_id=1, source_target_pairs={{0,8},{1,9},{2,10},{3,11},{4,12},{5,13},{6,14},{7,15},{8,0},{9,1},... | collective-permute-start | bytes 98312 | tf_op jit(solution)/shard_map/ppermute | solution.py:237
  27.6 2.1 %codes_step.3 = (bf16[64,128,256]{2,1,0:T(8,128)(2,1)}, bf16[64,256]{1,0:T(8,128)(2,1)S(1)}) custom-call(bf16[64,256]{1,0:T(8,128)(2,1)S(1)} %add_convert_fusion.sum_ref, bf16[64,128,256]{2,1,0:T(8,128)(2,1)S(1)} %get-tuple-element.14.codes_ref, bf16[64,16,512]{2,1,0:T(8,128)(2,1)S(1)} %get-tuple-element.20.shifted_ref, ...), custom_call_target="tpu_custom_call", output_to_operand_aliasing={{0}: (4, {})} | custom-call | flops 469762048 | bytes 3670016 | tf_op jit(solution)/shard_map/codes_step/pallas_call | solution.py:183
  29.8 0.1 collective-permute-done.6.last_ref
  29.9 0.1 normalize.1.mine_ref
  30.0 0.1 collective-permute-start.7
  30.1 1.2 %collective-permute-done.7.other_ref = f32[64,256]{1,0:T(8,128)S(1)} collective-permute-done((f32[64,256]{1,0:T(8,128)S(1)}, f32[64,256]{1,0:T(8,128)S(1)}, u32[]{:S(2)}, u32[]{:S(2)}) %collective-permute-start.7) | collective-permute-done | bytes 65568 | tf_op jit(solution)/shard_map/ppermute | solution.py:237
  31.3 0.7 %join.1 = f32[128,256]{1,0:T(8,128)} custom-call(f32[64,256]{1,0:T(8,128)S(1)} %normalize.1.mine_ref, f32[64,256]{1,0:T(8,128)S(1)} %collective-permute-done.7.other_ref), custom_call_target="tpu_custom_call" | custom-call | tf_op jit(solution)/shard_map/join/pallas_call | solution.py:311
  (2 shorter events, 0.0 us)
Async XLA Ops:
  6.0 1.4 %collective-permute-start = (f32[64,256]{1,0:T(8,128)S(1)}, f32[64,256]{1,0:T(8,128)S(1)}, u32[]{:S(2)}, u32[]{:S(2)}) collective-permute-start(f32[64,256]{1,0:T(8,128)S(1)} %get-tuple-element.15.sent_near_ref), channel_id=1, source_target_pairs={{0,1},{1,0},{2,3},{3,2},{4,5},{5,4},{6,7},{7,6},{8,9},{9,8},{10,11... | collective-permute-start | bytes 196616 | tf_op jit(solution)/shard_map/ppermute | solution.py:237
  6.5 0.7 %collective-permute-start.1 = (bf16[64,256]{1,0:T(8,128)(2,1)S(1)}, bf16[64,256]{1,0:T(8,128)(2,1)S(1)}, u32[]{:S(2)}, u32[]{:S(2)}) collective-permute-start(bf16[64,256]{1,0:T(8,128)(2,1)S(1)} %get-tuple-element.17), channel_id=1, source_target_pairs={{1,2},{3,4},{5,6},{7,8},{9,10},{11,12},{13,14},{2,1},{4,3},{6,5},{... | collective-permute-start | bytes 98312 | tf_op jit(solution)/shard_map/ppermute | solution.py:272
  10.3 6.2 %collective-permute-start.2 = (f32[64,256]{1,0:T(8,128)S(1)}, f32[64,256]{1,0:T(8,128)S(1)}, u32[]{:S(2)}, u32[]{:S(2)}) collective-permute-start(f32[64,256]{1,0:T(8,128)S(1)} %get-tuple-element.19), channel_id=1, source_target_pairs={{0,1},{1,0},{2,3},{3,2},{4,5},{5,4},{6,7},{7,6},{8,9},{9,8},{10,11... | collective-permute-start | bytes 196616 | tf_op jit(solution)/shard_map/ppermute | solution.py:237
  16.5 7.2 %collective-permute-start.5 = (bf16[64,256]{1,0:T(8,128)(2,1)S(1)}, bf16[64,256]{1,0:T(8,128)(2,1)S(1)}, u32[]{:S(2)}, u32[]{:S(2)}) collective-permute-start(bf16[64,256]{1,0:T(8,128)(2,1)S(1)} %add_convert_fusion.1.sum_ref), channel_id=1, source_target_pairs={{0,6},{1,7},{2,4},{3,5},{4,2},{5,3},{6,0},{7,1},{8,14},{9,15},{10,... | collective-permute-start | bytes 98312 | tf_op jit(solution)/shard_map/ppermute | solution.py:237
  20.6 3.9 %collective-permute-start.4 = (bf16[64,256]{1,0:T(8,128)(2,1)S(1)}, bf16[64,256]{1,0:T(8,128)(2,1)S(1)}, u32[]{:S(2)}, u32[]{:S(2)}) collective-permute-start(bf16[64,256]{1,0:T(8,128)(2,1)S(1)} %add_convert_fusion.1.sum_ref), channel_id=1, source_target_pairs={{0,4},{1,5},{2,6},{3,7},{4,0},{5,1},{6,2},{7,3},{8,12},{9,13},{10,... | collective-permute-start | bytes 98312 | tf_op jit(solution)/shard_map/ppermute | solution.py:237
  21.1 3.9 %collective-permute-start.3 = (bf16[64,256]{1,0:T(8,128)(2,1)S(1)}, bf16[64,256]{1,0:T(8,128)(2,1)S(1)}, u32[]{:S(2)}, u32[]{:S(2)}) collective-permute-start(bf16[64,256]{1,0:T(8,128)(2,1)S(1)} %add_convert_fusion.1.sum_ref), channel_id=1, source_target_pairs={{0,2},{1,3},{2,0},{3,1},{4,6},{5,7},{6,4},{7,5},{8,10},{9,11},{10,... | collective-permute-start | bytes 98312 | tf_op jit(solution)/shard_map/ppermute | solution.py:237
  25.0 4.9 %collective-permute-start.6 = (bf16[64,256]{1,0:T(8,128)(2,1)S(1)}, bf16[64,256]{1,0:T(8,128)(2,1)S(1)}, u32[]{:S(2)}, u32[]{:S(2)}) collective-permute-start(bf16[64,256]{1,0:T(8,128)(2,1)S(1)} %add_convert_fusion.sum_ref), channel_id=1, source_target_pairs={{0,8},{1,9},{2,10},{3,11},{4,12},{5,13},{6,14},{7,15},{8,0},{9,1},... | collective-permute-start | bytes 98312 | tf_op jit(solution)/shard_map/ppermute | solution.py:237
  30.0 1.3 %collective-permute-start.7 = (f32[64,256]{1,0:T(8,128)S(1)}, f32[64,256]{1,0:T(8,128)S(1)}, u32[]{:S(2)}, u32[]{:S(2)}) collective-permute-start(f32[64,256]{1,0:T(8,128)S(1)} %normalize.1.mine_ref), channel_id=1, source_target_pairs={{0,1},{1,0},{2,3},{3,2},{4,5},{5,4},{6,7},{7,6},{8,9},{9,8},{10,11... | collective-permute-start | bytes 196616 | tf_op jit(solution)/shard_map/ppermute | solution.py:237

commit v5 on v4

--- a/solution.py
+++ b/solution.py
@@ -19,11 +19,12 @@
 GROUP = 8
 CHUNKS = 3
 PACK = 16
+PITCH = 17
 VMEM_BYTES = 5 << 20
 
 
 def chunk_starts(chans):
-    return [0, chans // 8, 3 * chans // 8, chans]
+    return [0, chans // 4, chans // 2, chans]
 
 
 def fetch_parts(source, target, arrived, starts):
@@ -71,42 +72,54 @@
         ],
         axis=0,
     )
-    lane = lane_index((8, LANES))
-    for c in range(0, chans, 2):
-        if c in fetches:
-            fetches[c].wait()
-        pair = [codes_ref[c], codes_ref[c + 1]]
-        halves = [jnp.concatenate([x[:, n * LANES : (n + 1) * LANES] for x in pair], axis=1) for n in range(2)]
-        terms = jnp.dot(dict_rows, jnp.concatenate(halves, axis=0), preferred_element_type=F32)
-        for j in range(2):
-            sums = [None] * 4
-            for m in range(LANES // 8):
-                diagonals = [
-                    terms[n * LANES + 8 * m : n * LANES + 8 * m + 8, j * LANES : (j + 1) * LANES] for n in range(3)
-                ]
-                if m == 0:
-                    sums = diagonals + [jnp.zeros((8, LANES), F32)]
-                    continue
-                turned = [pltpu.roll(d, 8 * m, 1) for d in diagonals]
-                inside = lane >= 8 * m
-                sums[0] += jnp.where(inside, turned[0], 0.0)
-                sums[1] += jnp.where(inside, turned[1], turned[0])
-                sums[2] += jnp.where(inside, turned[2], turned[1])
-                sums[3] += jnp.where(inside, 0.0, turned[2])
-            for n in range(4):
-                shear_ref[n, 8 * (c + j) : 8 * (c + j) + 8, :] = sums[n]
-    total = jnp.zeros((chans, 4 * LANES), F32)
-    for r in range(8):
-        row = jnp.concatenate([shear_ref[n, pl.ds(r, chans, stride=8), :] for n in range(4)], axis=1)
-        total += pltpu.roll(row, r, 1) if r else row
-    signal_in.wait()
-    own = total[:, :taps] - signal_ref[...].astype(F32)
-    onward = total[:, taps:]
+    lane = lane_index((PACK, LANES))
+    zero = jnp.zeros((PACK, LANES), BF16)
     even = parity() == 0
-    near_ref[...] = jnp.where(even, onward, own)
-    far = jnp.where(even, own, onward)
-    far_ref[...] = far
-    far_sent_ref[...] = far.astype(far_sent_ref.dtype)
+
+    def finish(first):
+        total = jnp.zeros((PACK, 4 * LANES), F32)
+        for r in range(PACK):
+            parts = [shear_ref[n, pl.ds(PITCH * first + r, PACK, stride=PITCH), :] for n in range(4)]
+            row = jnp.concatenate(parts, axis=1)
+            total += pltpu.roll(row, r, 1) if r else row
+        rows = slice(first, first + PACK)
+        own = total[:, :taps] - signal_ref[rows, :].astype(F32)
+        onward = total[:, taps:]
+        near_ref[rows, :] = jnp.where(even, onward, own)
+        far = jnp.where(even, own, onward)
+        far_ref[rows, :] = far
+        far_sent_ref[rows, :] = far.astype(far_sent_ref.dtype)
+
+    for first in range(0, chans, PACK):
+        if first == PACK:
+            signal_in.wait()
+        for c in range(first, first + PACK, 2):
+            if c in fetches:
+                fetches[c].wait()
+            pair = [codes_ref[c], codes_ref[c + 1]]
+            halves = [jnp.concatenate([x[:, n * LANES : (n + 1) * LANES] for x in pair], axis=1) for n in range(2)]
+            terms = jnp.dot(dict_rows, jnp.concatenate(halves, axis=0), preferred_element_type=F32).astype(BF16)
+            for j in range(2):
+                sums = [None] * 4
+                for m in range(LANES // PACK):
+                    diagonals = [
+                        terms[n * LANES + PACK * m : n * LANES + PACK * (m + 1), j * LANES : (j + 1) * LANES]
+                        for n in range(3)
+                    ]
+                    if m == 0:
+                        sums = [d.astype(F32) for d in diagonals] + [jnp.zeros((PACK, LANES), F32)]
+                        continue
+                    turned = [pltpu.roll(d, PACK * m, 1) for d in diagonals]
+                    inside = lane >= PACK * m
+                    sums[0] += jnp.where(inside, turned[0], zero).astype(F32)
+                    sums[1] += jnp.where(inside, turned[1], turned[0]).astype(F32)
+                    sums[2] += jnp.where(inside, turned[2], turned[1]).astype(F32)
+                    sums[3] += jnp.where(inside, zero, turned[2]).astype(F32)
+                for n in range(4):
+                    shear_ref[n, PITCH * (c + j) : PITCH * (c + j) + PACK, :] = sums[n]
+        if first:
+            finish(first - PACK)
+    finish(chans - PACK)
 
 
 def hankel_block(shifted, lane):
@@ -144,9 +157,9 @@
         for r in range(PACK):
             moved = (pltpu.roll(rows, width - r, 1) if r else rows).astype(F32)
             for n in range(4):
-                wide_ref[n, pl.ds(first * PACK + r, PACK, stride=PACK), :] = moved[:, n * LANES : (n + 1) * LANES]
+                wide_ref[n, pl.ds(first * PITCH + r, PACK, stride=PITCH), :] = moved[:, n * LANES : (n + 1) * LANES]
         for c in range(first, first + PACK):
-            rows_c = pl.ds(c * PACK, PACK)
+            rows_c = pl.ds(c * PITCH, PACK)
             shifted = jnp.concatenate([wide_ref[n, rows_c, :] for n in range(4)], axis=1).astype(BF16)
             shifted_ref[c] = shifted
             total += jnp.dot(codes_ref[c], hankel_block(shifted, lane), preferred_element_type=F32)
@@ -258,7 +271,7 @@
         ],
         scratch_shapes=[
             pltpu.VMEM(signal.shape, BF16),
-            pltpu.VMEM((4, 8 * chans, LANES), F32),
+            pltpu.VMEM((4, PITCH * (chans + 1), LANES), F32),
             pltpu.SemaphoreType.DMA((CHUNKS,)),
             pltpu.SemaphoreType.DMA((2,)),
         ],
@@ -281,7 +294,7 @@
             jax.ShapeDtypeStruct((half, taps), F32),
             jax.ShapeDtypeStruct((chans, PACK, 2 * taps), BF16),
         ],
-        scratch_shapes=[pltpu.VMEM((4, chans * PACK, LANES), F32)],
+        scratch_shapes=[pltpu.VMEM((4, PITCH * (chans + 1), LANES), F32)],
         compiler_params=params,
         cost_estimate=pl.CostEstimate(flops=matmul_flops, bytes_accessed=codes.size * 2, transcendentals=0),
         name="dict_grad",

time: 32.1 us -> 30.5 us (0.950)
  Pallas kernels: 13.7 us -> 12 us
    pallas_call x1, Pallas kernels: 5.36 us -> 4.3 us  [shards(): pl.pallas_call(spread_kernel, in_specs=[in_hbm()] * 3, out_specs=[in_vmem...]
    pallas_call x1, Pallas kernels: 2.87 us -> 2.31 us  [shards(): pl.pallas_call(dict_kernel, in_specs=[in_vmem()] * 5, out_specs=[in_vmem(...]
where the time goes in v5:
time: 30.5 us; the launch traced here: 30.3 us
  starting transfers between devices  13.9 us (46%)
  Pallas kernels  12 us (39%)
  waiting for transfers between devices  3.68 us (12%)
  between operations  0.71 us (2%)
    ppermute x7, starting transfers between devices, exchange(): return lax.ppermute(block, 'tm', [(i, i ^ distance) for i in range(size)])  13.3 us
    pallas_call x2, Pallas kernels, step_codes(): pl.pallas_call(functools.partial(codes_kernel, first), in_specs=[in_vmem(...  4.64 us
    pallas_call x1, Pallas kernels, shards(): pl.pallas_call(spread_kernel, in_specs=[in_hbm()] * 3, out_specs=[in_vmem...  4.3 us
    ppermute x7, waiting for transfers between devices, exchange(): return lax.ppermute(block, 'tm', [(i, i ^ distance) for i in range(size)])  3.67 us
    pallas_call x1, Pallas kernels, shards(): pl.pallas_call(dict_kernel, in_specs=[in_vmem()] * 5, out_specs=[in_vmem(...  2.31 us
    pallas_call x1, Pallas kernels, shards(): pl.pallas_call(join_kernel, in_specs=[in_vmem()] * 2, out_specs=in_vmem()...  0.67 us
    ppermute x1, starting transfers between devices, shards(): got_far = lax.ppermute(sent_far, 'tm', across)  0.65 us
  transfers between devices with their start and end apart: 8, of which 6 were waited for; matrix products, arithmetic and copies ran while one was open for 0% of the time, Pallas kernels for 15%

profile of v5, /device:TPU:0, one launch (start us, length us, event | category | flops | bytes accessed | tf_op | source)
XLA Modules:
  0.0 30.3 jit_solution(15420812179027173127)
XLA Ops:
  0.6 4.3 %spread.1 = (bf16[64,128,256]{2,1,0:T(8,128)(2,1)S(1)}, f32[128,256]{1,0:T(8,128)S(1)}, f32[64,256]{1,0:T(8,128)S(1)}, bf16[64,256]{1,0:T(8,128)(2,1)S(1)}, f32[64,256]{1,0:T(8,128)S(1)}) custom-call(bf16[64,128,256]{2,1,0:T(8,128)(2,1)} %codes_hbm.1, bf16[64,256]{1,0:T(8,128)(2,1)} %signal_hbm.1, f32[128,256]{1,0:T(8,128)} %filters_hbm.1), custom_call_target="tpu_custom_call" | custom-call | flops 1073741824 | bytes 4194304 | tf_op jit(solution)/shard_map/spread/pallas_call | solution.py:261
  4.9 0.5 %collective-permute-start = (f32[64,256]{1,0:T(8,128)S(1)}, f32[64,256]{1,0:T(8,128)S(1)}, u32[]{:S(2)}, u32[]{:S(2)}) collective-permute-start(f32[64,256]{1,0:T(8,128)S(1)} %get-tuple-element.15.sent_near_ref), channel_id=1, source_target_pairs={{0,1},{1,0},{2,3},{3,2},{4,5},{5,4},{6,7},{7,6},{8,9},{9,8},{10,11... | collective-permute-start | bytes 196616 | tf_op jit(solution)/shard_map/ppermute | solution.py:250
  5.5 0.7 %collective-permute-start.1 = (bf16[64,256]{1,0:T(8,128)(2,1)S(1)}, bf16[64,256]{1,0:T(8,128)(2,1)S(1)}, u32[]{:S(2)}, u32[]{:S(2)}) collective-permute-start(bf16[64,256]{1,0:T(8,128)(2,1)S(1)} %get-tuple-element.17), channel_id=1, source_target_pairs={{1,2},{3,4},{5,6},{7,8},{9,10},{11,12},{13,14},{2,1},{4,3},{6,5},{... | collective-permute-start | bytes 98312 | tf_op jit(solution)/shard_map/ppermute | solution.py:285
  6.1 0.0 collective-permute-done.1.got_far_ref
  6.1 0.2 collective-permute-done.got_near_ref
  6.4 2.3 %dict_grad.1 = (f32[64,256]{1,0:T(8,128)S(1)}, f32[64,256]{1,0:T(8,128)S(1)}, bf16[64,16,512]{2,1,0:T(8,128)(2,1)S(1)}) custom-call(bf16[64,128,256]{2,1,0:T(8,128)(2,1)S(1)} %get-tuple-element.14.codes_ref, f32[64,256]{1,0:T(8,128)S(1)} %get-tuple-element.15.sent_near_ref, f32[64,256]{1,0:T(8,128)S(1)} %get-tuple-element.16.sent_far_ref, ...), custom_call_target="tpu_custom_call" | custom-call | flops 1073741824 | bytes 4194304 | tf_op jit(solution)/shard_map/dict_grad/pallas_call | solution.py:288
  8.7 5.3 %collective-permute-start.2 = (f32[64,256]{1,0:T(8,128)S(1)}, f32[64,256]{1,0:T(8,128)S(1)}, u32[]{:S(2)}, u32[]{:S(2)}) collective-permute-start(f32[64,256]{1,0:T(8,128)S(1)} %get-tuple-element.19), channel_id=1, source_target_pairs={{0,1},{1,0},{2,3},{3,2},{4,5},{5,4},{6,7},{7,6},{8,9},{9,8},{10,11... | collective-permute-start | bytes 196616 | tf_op jit(solution)/shard_map/ppermute | solution.py:250
  14.0 0.9 %collective-permute-done.2 = f32[64,256]{1,0:T(8,128)S(1)} collective-permute-done((f32[64,256]{1,0:T(8,128)S(1)}, f32[64,256]{1,0:T(8,128)S(1)}, u32[]{:S(2)}, u32[]{:S(2)}) %collective-permute-start.2) | collective-permute-done | bytes 65568 | tf_op jit(solution)/shard_map/ppermute | solution.py:250
  14.9 4.1 %collective-permute-start.5 = (bf16[64,256]{1,0:T(8,128)(2,1)S(1)}, bf16[64,256]{1,0:T(8,128)(2,1)S(1)}, u32[]{:S(2)}, u32[]{:S(2)}) collective-permute-start(bf16[64,256]{1,0:T(8,128)(2,1)S(1)} %add_convert_fusion.1.sum_ref), channel_id=1, source_target_pairs={{0,6},{1,7},{2,4},{3,5},{4,2},{5,3},{6,0},{7,1},{8,14},{9,15},{10,... | collective-permute-start | bytes 98312 | tf_op jit(solution)/shard_map/ppermute | solution.py:250
  19.0 0.5 %collective-permute-start.4 = (bf16[64,256]{1,0:T(8,128)(2,1)S(1)}, bf16[64,256]{1,0:T(8,128)(2,1)S(1)}, u32[]{:S(2)}, u32[]{:S(2)}) collective-permute-start(bf16[64,256]{1,0:T(8,128)(2,1)S(1)} %add_convert_fusion.1.sum_ref), channel_id=1, source_target_pairs={{0,4},{1,5},{2,6},{3,7},{4,0},{5,1},{6,2},{7,3},{8,12},{9,13},{10,... | collective-permute-start | bytes 98312 | tf_op jit(solution)/shard_map/ppermute | solution.py:250
  19.4 0.2 collective-permute-start.3
  19.6 2.5 %codes_step.2 = (bf16[64,128,256]{2,1,0:T(8,128)(2,1)}, bf16[64,256]{1,0:T(8,128)(2,1)S(1)}) custom-call(bf16[64,256]{1,0:T(8,128)(2,1)S(1)} %add_convert_fusion.1.sum_ref, bf16[64,128,256]{2,1,0:T(8,128)(2,1)S(1)} %get-tuple-element.14.codes_ref, bf16[64,16,512]{2,1,0:T(8,128)(2,1)S(1)} %get-tuple-element.20.shifted_ref, ...), custom_call_target="tpu_custom_call" | custom-call | flops 603979776 | bytes 4718592 | tf_op jit(solution)/shard_map/codes_step/pallas_call | solution.py:196
  22.1 0.0 collective-permute-done.5
  22.1 0.8 %collective-permute-done.4 = bf16[64,256]{1,0:T(8,128)(2,1)S(1)} collective-permute-done((bf16[64,256]{1,0:T(8,128)(2,1)S(1)}, bf16[64,256]{1,0:T(8,128)(2,1)S(1)}, u32[]{:S(2)}, u32[]{:S(2)}) %collective-permute-start.4) | collective-permute-done | bytes 32800 | tf_op jit(solution)/shard_map/ppermute | solution.py:250
  22.9 0.5 %collective-permute-done.3 = bf16[64,256]{1,0:T(8,128)(2,1)S(1)} collective-permute-done((bf16[64,256]{1,0:T(8,128)(2,1)S(1)}, bf16[64,256]{1,0:T(8,128)(2,1)S(1)}, u32[]{:S(2)}, u32[]{:S(2)}) %collective-permute-start.3) | collective-permute-done | bytes 32800 | tf_op jit(solution)/shard_map/ppermute | solution.py:250
  23.4 2.6 %collective-permute-start.6 = (bf16[64,256]{1,0:T(8,128)(2,1)S(1)}, bf16[64,256]{1,0:T(8,128)(2,1)S(1)}, u32[]{:S(2)}, u32[]{:S(2)}) collective-permute-start(bf16[64,256]{1,0:T(8,128)(2,1)S(1)} %add_convert_fusion.sum_ref), channel_id=1, source_target_pairs={{0,8},{1,9},{2,10},{3,11},{4,12},{5,13},{6,14},{7,15},{8,0},{9,1},... | collective-permute-start | bytes 98312 | tf_op jit(solution)/shard_map/ppermute | solution.py:250
  26.0 2.1 %codes_step.3 = (bf16[64,128,256]{2,1,0:T(8,128)(2,1)}, bf16[64,256]{1,0:T(8,128)(2,1)S(1)}) custom-call(bf16[64,256]{1,0:T(8,128)(2,1)S(1)} %add_convert_fusion.sum_ref, bf16[64,128,256]{2,1,0:T(8,128)(2,1)S(1)} %get-tuple-element.14.codes_ref, bf16[64,16,512]{2,1,0:T(8,128)(2,1)S(1)} %get-tuple-element.20.shifted_ref, ...), custom_call_target="tpu_custom_call", output_to_operand_aliasing={{0}: (4, {})} | custom-call | flops 469762048 | bytes 3670016 | tf_op jit(solution)/shard_map/codes_step/pallas_call | solution.py:196
  28.2 0.1 collective-permute-done.6.last_ref
  28.2 0.1 normalize.1.mine_ref
  28.4 0.1 collective-permute-start.7
  28.4 1.2 %collective-permute-done.7.other_ref = f32[64,256]{1,0:T(8,128)S(1)} collective-permute-done((f32[64,256]{1,0:T(8,128)S(1)}, f32[64,256]{1,0:T(8,128)S(1)}, u32[]{:S(2)}, u32[]{:S(2)}) %collective-permute-start.7) | collective-permute-done | bytes 65568 | tf_op jit(solution)/shard_map/ppermute | solution.py:250
  29.7 0.7 %join.1 = f32[128,256]{1,0:T(8,128)} custom-call(f32[64,256]{1,0:T(8,128)S(1)} %normalize.1.mine_ref, f32[64,256]{1,0:T(8,128)S(1)} %collective-permute-done.7.other_ref), custom_call_target="tpu_custom_call" | custom-call | tf_op jit(solution)/shard_map/join/pallas_call | solution.py:324
  (2 shorter events, 0.0 us)
Async XLA Ops:
  4.9 1.4 %collective-permute-start = (f32[64,256]{1,0:T(8,128)S(1)}, f32[64,256]{1,0:T(8,128)S(1)}, u32[]{:S(2)}, u32[]{:S(2)}) collective-permute-start(f32[64,256]{1,0:T(8,128)S(1)} %get-tuple-element.15.sent_near_ref), channel_id=1, source_target_pairs={{0,1},{1,0},{2,3},{3,2},{4,5},{5,4},{6,7},{7,6},{8,9},{9,8},{10,11... | collective-permute-start | bytes 196616 | tf_op jit(solution)/shard_map/ppermute | solution.py:250
  5.5 0.7 %collective-permute-start.1 = (bf16[64,256]{1,0:T(8,128)(2,1)S(1)}, bf16[64,256]{1,0:T(8,128)(2,1)S(1)}, u32[]{:S(2)}, u32[]{:S(2)}) collective-permute-start(bf16[64,256]{1,0:T(8,128)(2,1)S(1)} %get-tuple-element.17), channel_id=1, source_target_pairs={{1,2},{3,4},{5,6},{7,8},{9,10},{11,12},{13,14},{2,1},{4,3},{6,5},{... | collective-permute-start | bytes 98312 | tf_op jit(solution)/shard_map/ppermute | solution.py:285
  8.7 6.2 %collective-permute-start.2 = (f32[64,256]{1,0:T(8,128)S(1)}, f32[64,256]{1,0:T(8,128)S(1)}, u32[]{:S(2)}, u32[]{:S(2)}) collective-permute-start(f32[64,256]{1,0:T(8,128)S(1)} %get-tuple-element.19), channel_id=1, source_target_pairs={{0,1},{1,0},{2,3},{3,2},{4,5},{5,4},{6,7},{7,6},{8,9},{9,8},{10,11... | collective-permute-start | bytes 196616 | tf_op jit(solution)/shard_map/ppermute | solution.py:250
  14.9 7.2 %collective-permute-start.5 = (bf16[64,256]{1,0:T(8,128)(2,1)S(1)}, bf16[64,256]{1,0:T(8,128)(2,1)S(1)}, u32[]{:S(2)}, u32[]{:S(2)}) collective-permute-start(bf16[64,256]{1,0:T(8,128)(2,1)S(1)} %add_convert_fusion.1.sum_ref), channel_id=1, source_target_pairs={{0,6},{1,7},{2,4},{3,5},{4,2},{5,3},{6,0},{7,1},{8,14},{9,15},{10,... | collective-permute-start | bytes 98312 | tf_op jit(solution)/shard_map/ppermute | solution.py:250
  19.0 3.9 %collective-permute-start.4 = (bf16[64,256]{1,0:T(8,128)(2,1)S(1)}, bf16[64,256]{1,0:T(8,128)(2,1)S(1)}, u32[]{:S(2)}, u32[]{:S(2)}) collective-permute-start(bf16[64,256]{1,0:T(8,128)(2,1)S(1)} %add_convert_fusion.1.sum_ref), channel_id=1, source_target_pairs={{0,4},{1,5},{2,6},{3,7},{4,0},{5,1},{6,2},{7,3},{8,12},{9,13},{10,... | collective-permute-start | bytes 98312 | tf_op jit(solution)/shard_map/ppermute | solution.py:250
  19.4 3.9 %collective-permute-start.3 = (bf16[64,256]{1,0:T(8,128)(2,1)S(1)}, bf16[64,256]{1,0:T(8,128)(2,1)S(1)}, u32[]{:S(2)}, u32[]{:S(2)}) collective-permute-start(bf16[64,256]{1,0:T(8,128)(2,1)S(1)} %add_convert_fusion.1.sum_ref), channel_id=1, source_target_pairs={{0,2},{1,3},{2,0},{3,1},{4,6},{5,7},{6,4},{7,5},{8,10},{9,11},{10,... | collective-permute-start | bytes 98312 | tf_op jit(solution)/shard_map/ppermute | solution.py:250
  23.4 4.9 %collective-permute-start.6 = (bf16[64,256]{1,0:T(8,128)(2,1)S(1)}, bf16[64,256]{1,0:T(8,128)(2,1)S(1)}, u32[]{:S(2)}, u32[]{:S(2)}) collective-permute-start(bf16[64,256]{1,0:T(8,128)(2,1)S(1)} %add_convert_fusion.sum_ref), channel_id=1, source_target_pairs={{0,8},{1,9},{2,10},{3,11},{4,12},{5,13},{6,14},{7,15},{8,0},{9,1},... | collective-permute-start | bytes 98312 | tf_op jit(solution)/shard_map/ppermute | solution.py:250
  28.4 1.3 %collective-permute-start.7 = (f32[64,256]{1,0:T(8,128)S(1)}, f32[64,256]{1,0:T(8,128)S(1)}, u32[]{:S(2)}, u32[]{:S(2)}) collective-permute-start(f32[64,256]{1,0:T(8,128)S(1)} %normalize.1.mine_ref), channel_id=1, source_target_pairs={{0,1},{1,0},{2,3},{3,2},{4,5},{5,4},{6,7},{7,6},{8,9},{9,8},{10,11... | collective-permute-start | bytes 196616 | tf_op jit(solution)/shard_map/ppermute | solution.py:250

commit v6 on v5

--- a/solution.py
+++ b/solution.py
@@ -20,6 +20,8 @@
 CHUNKS = 3
 PACK = 16
 PITCH = 17
+SUMS = 8
+SUM_PITCH = 9
 VMEM_BYTES = 5 << 20
 
 
@@ -78,8 +80,8 @@
 
     def finish(first):
         total = jnp.zeros((PACK, 4 * LANES), F32)
-        for r in range(PACK):
-            parts = [shear_ref[n, pl.ds(PITCH * first + r, PACK, stride=PITCH), :] for n in range(4)]
+        for r in range(SUMS):
+            parts = [shear_ref[n, pl.ds(SUM_PITCH * first + r, PACK, stride=SUM_PITCH), :] for n in range(4)]
             row = jnp.concatenate(parts, axis=1)
             total += pltpu.roll(row, r, 1) if r else row
         rows = slice(first, first + PACK)
@@ -98,25 +100,26 @@
                 fetches[c].wait()
             pair = [codes_ref[c], codes_ref[c + 1]]
             halves = [jnp.concatenate([x[:, n * LANES : (n + 1) * LANES] for x in pair], axis=1) for n in range(2)]
-            terms = jnp.dot(dict_rows, jnp.concatenate(halves, axis=0), preferred_element_type=F32).astype(BF16)
+            terms = jnp.dot(dict_rows, jnp.concatenate(halves, axis=0), preferred_element_type=F32)
+            sums = [None] * 4
+            for m in range(LANES // SUMS):
+                diagonals = []
+                for n in range(3):
+                    rows = terms[n * LANES + SUMS * m : n * LANES + SUMS * (m + 1)]
+                    diagonals.append(jnp.concatenate([rows[:, :LANES], rows[:, LANES:]], axis=0))
+                if m == 0:
+                    sums = diagonals + [jnp.zeros((2 * SUMS, LANES), F32)]
+                    continue
+                turned = [pltpu.roll(d.astype(BF16), SUMS * m, 1) for d in diagonals]
+                inside = lane >= SUMS * m
+                sums[0] += jnp.where(inside, turned[0], zero).astype(F32)
+                sums[1] += jnp.where(inside, turned[1], turned[0]).astype(F32)
+                sums[2] += jnp.where(inside, turned[2], turned[1]).astype(F32)
+                sums[3] += jnp.where(inside, zero, turned[2]).astype(F32)
             for j in range(2):
-                sums = [None] * 4
-                for m in range(LANES // PACK):
-                    diagonals = [
-                        terms[n * LANES + PACK * m : n * LANES + PACK * (m + 1), j * LANES : (j + 1) * LANES]
-                        for n in range(3)
-                    ]
-                    if m == 0:
-                        sums = [d.astype(F32) for d in diagonals] + [jnp.zeros((PACK, LANES), F32)]
-                        continue
-                    turned = [pltpu.roll(d, PACK * m, 1) for d in diagonals]
-                    inside = lane >= PACK * m
-                    sums[0] += jnp.where(inside, turned[0], zero).astype(F32)
-                    sums[1] += jnp.where(inside, turned[1], turned[0]).astype(F32)
-                    sums[2] += jnp.where(inside, turned[2], turned[1]).astype(F32)
-                    sums[3] += jnp.where(inside, zero, turned[2]).astype(F32)
                 for n in range(4):
-                    shear_ref[n, PITCH * (c + j) : PITCH * (c + j) + PACK, :] = sums[n]
+                    place = SUM_PITCH * (c + j)
+                    shear_ref[n, place : place + SUMS, :] = sums[n][SUMS * j : SUMS * (j + 1)]
         if first:
             finish(first - PACK)
     finish(chans - PACK)
@@ -271,7 +274,7 @@
         ],
         scratch_shapes=[
             pltpu.VMEM(signal.shape, BF16),
-            pltpu.VMEM((4, PITCH * (chans + 1), LANES), F32),
+            pltpu.VMEM((4, SUM_PITCH * (chans + 1), LANES), F32),
             pltpu.SemaphoreType.DMA((CHUNKS,)),
             pltpu.SemaphoreType.DMA((2,)),
         ],

time: 30.5 us -> 30.4 us (level)
  no operation moved by 1% of the time
where the time goes in v6:
time: 30.4 us; the launch traced here: 30.3 us
  starting transfers between devices  13.9 us (46%)
  Pallas kernels  11.9 us (39%)
  waiting for transfers between devices  3.66 us (12%)
  between operations  0.71 us (2%)
    ppermute x7, starting transfers between devices, exchange(): return lax.ppermute(block, 'tm', [(i, i ^ distance) for i in range(size)])  13.3 us
    pallas_call x2, Pallas kernels, step_codes(): pl.pallas_call(functools.partial(codes_kernel, first), in_specs=[in_vmem(...  4.64 us
    pallas_call x1, Pallas kernels, shards(): pl.pallas_call(spread_kernel, in_specs=[in_hbm()] * 3, out_specs=[in_vmem...  4.21 us
    ppermute x7, waiting for transfers between devices, exchange(): return lax.ppermute(block, 'tm', [(i, i ^ distance) for i in range(size)])  3.66 us
    pallas_call x1, Pallas kernels, shards(): pl.pallas_call(dict_kernel, in_specs=[in_vmem()] * 5, out_specs=[in_vmem(...  2.3 us
    pallas_call x1, Pallas kernels, shards(): pl.pallas_call(join_kernel, in_specs=[in_vmem()] * 2, out_specs=in_vmem()...  0.67 us
    ppermute x1, starting transfers between devices, shards(): got_far = lax.ppermute(sent_far, 'tm', across)  0.65 us
  transfers between devices with their start and end apart: 8, of which 6 were waited for; matrix products, arithmetic and copies ran while one was open for 0% of the time, Pallas kernels for 15%

profile of v6, /device:TPU:0, one launch (start us, length us, event | category | flops | bytes accessed | tf_op | source)
XLA Modules:
  0.0 30.3 jit_solution(13683953608991607179)
XLA Ops:
  0.6 4.2 %spread.1 = (bf16[64,128,256]{2,1,0:T(8,128)(2,1)S(1)}, f32[128,256]{1,0:T(8,128)S(1)}, f32[64,256]{1,0:T(8,128)S(1)}, bf16[64,256]{1,0:T(8,128)(2,1)S(1)}, f32[64,256]{1,0:T(8,128)S(1)}) custom-call(bf16[64,128,256]{2,1,0:T(8,128)(2,1)} %codes_hbm.1, bf16[64,256]{1,0:T(8,128)(2,1)} %signal_hbm.1, f32[128,256]{1,0:T(8,128)} %filters_hbm.1), custom_call_target="tpu_custom_call" | custom-call | flops 1073741824 | bytes 4194304 | tf_op jit(solution)/shard_map/spread/pallas_call | solution.py:264
  4.8 0.5 %collective-permute-start = (f32[64,256]{1,0:T(8,128)S(1)}, f32[64,256]{1,0:T(8,128)S(1)}, u32[]{:S(2)}, u32[]{:S(2)}) collective-permute-start(f32[64,256]{1,0:T(8,128)S(1)} %get-tuple-element.15.sent_near_ref), channel_id=1, source_target_pairs={{0,1},{1,0},{2,3},{3,2},{4,5},{5,4},{6,7},{7,6},{8,9},{9,8},{10,11... | collective-permute-start | bytes 196616 | tf_op jit(solution)/shard_map/ppermute | solution.py:253
  5.4 0.7 %collective-permute-start.1 = (bf16[64,256]{1,0:T(8,128)(2,1)S(1)}, bf16[64,256]{1,0:T(8,128)(2,1)S(1)}, u32[]{:S(2)}, u32[]{:S(2)}) collective-permute-start(bf16[64,256]{1,0:T(8,128)(2,1)S(1)} %get-tuple-element.17), channel_id=1, source_target_pairs={{1,2},{3,4},{5,6},{7,8},{9,10},{11,12},{13,14},{2,1},{4,3},{6,5},{... | collective-permute-start | bytes 98312 | tf_op jit(solution)/shard_map/ppermute | solution.py:288
  6.0 0.0 collective-permute-done.1.got_far_ref
  6.0 0.2 collective-permute-done.got_near_ref
  6.3 2.3 %dict_grad.1 = (f32[64,256]{1,0:T(8,128)S(1)}, f32[64,256]{1,0:T(8,128)S(1)}, bf16[64,16,512]{2,1,0:T(8,128)(2,1)S(1)}) custom-call(bf16[64,128,256]{2,1,0:T(8,128)(2,1)S(1)} %get-tuple-element.14.codes_ref, f32[64,256]{1,0:T(8,128)S(1)} %get-tuple-element.15.sent_near_ref, f32[64,256]{1,0:T(8,128)S(1)} %get-tuple-element.16.sent_far_ref, ...), custom_call_target="tpu_custom_call" | custom-call | flops 1073741824 | bytes 4194304 | tf_op jit(solution)/shard_map/dict_grad/pallas_call | solution.py:291
  8.6 5.3 %collective-permute-start.2 = (f32[64,256]{1,0:T(8,128)S(1)}, f32[64,256]{1,0:T(8,128)S(1)}, u32[]{:S(2)}, u32[]{:S(2)}) collective-permute-start(f32[64,256]{1,0:T(8,128)S(1)} %get-tuple-element.19), channel_id=1, source_target_pairs={{0,1},{1,0},{2,3},{3,2},{4,5},{5,4},{6,7},{7,6},{8,9},{9,8},{10,11... | collective-permute-start | bytes 196616 | tf_op jit(solution)/shard_map/ppermute | solution.py:253
  13.9 0.9 %collective-permute-done.2 = f32[64,256]{1,0:T(8,128)S(1)} collective-permute-done((f32[64,256]{1,0:T(8,128)S(1)}, f32[64,256]{1,0:T(8,128)S(1)}, u32[]{:S(2)}, u32[]{:S(2)}) %collective-permute-start.2) | collective-permute-done | bytes 65568 | tf_op jit(solution)/shard_map/ppermute | solution.py:253
  14.8 4.1 %collective-permute-start.5 = (bf16[64,256]{1,0:T(8,128)(2,1)S(1)}, bf16[64,256]{1,0:T(8,128)(2,1)S(1)}, u32[]{:S(2)}, u32[]{:S(2)}) collective-permute-start(bf16[64,256]{1,0:T(8,128)(2,1)S(1)} %add_convert_fusion.1.sum_ref), channel_id=1, source_target_pairs={{0,6},{1,7},{2,4},{3,5},{4,2},{5,3},{6,0},{7,1},{8,14},{9,15},{10,... | collective-permute-start | bytes 98312 | tf_op jit(solution)/shard_map/ppermute | solution.py:253
  18.9 0.4 %collective-permute-start.4 = (bf16[64,256]{1,0:T(8,128)(2,1)S(1)}, bf16[64,256]{1,0:T(8,128)(2,1)S(1)}, u32[]{:S(2)}, u32[]{:S(2)}) collective-permute-start(bf16[64,256]{1,0:T(8,128)(2,1)S(1)} %add_convert_fusion.1.sum_ref), channel_id=1, source_target_pairs={{0,4},{1,5},{2,6},{3,7},{4,0},{5,1},{6,2},{7,3},{8,12},{9,13},{10,... | collective-permute-start | bytes 98312 | tf_op jit(solution)/shard_map/ppermute | solution.py:253
  19.3 0.2 collective-permute-start.3
  19.5 2.5 %codes_step.2 = (bf16[64,128,256]{2,1,0:T(8,128)(2,1)}, bf16[64,256]{1,0:T(8,128)(2,1)S(1)}) custom-call(bf16[64,256]{1,0:T(8,128)(2,1)S(1)} %add_convert_fusion.1.sum_ref, bf16[64,128,256]{2,1,0:T(8,128)(2,1)S(1)} %get-tuple-element.14.codes_ref, bf16[64,16,512]{2,1,0:T(8,128)(2,1)S(1)} %get-tuple-element.20.shifted_ref, ...), custom_call_target="tpu_custom_call" | custom-call | flops 603979776 | bytes 4718592 | tf_op jit(solution)/shard_map/codes_step/pallas_call | solution.py:199
  22.0 0.0 collective-permute-done.5
  22.0 0.8 %collective-permute-done.4 = bf16[64,256]{1,0:T(8,128)(2,1)S(1)} collective-permute-done((bf16[64,256]{1,0:T(8,128)(2,1)S(1)}, bf16[64,256]{1,0:T(8,128)(2,1)S(1)}, u32[]{:S(2)}, u32[]{:S(2)}) %collective-permute-start.4) | collective-permute-done | bytes 32800 | tf_op jit(solution)/shard_map/ppermute | solution.py:253
  22.8 0.4 %collective-permute-done.3 = bf16[64,256]{1,0:T(8,128)(2,1)S(1)} collective-permute-done((bf16[64,256]{1,0:T(8,128)(2,1)S(1)}, bf16[64,256]{1,0:T(8,128)(2,1)S(1)}, u32[]{:S(2)}, u32[]{:S(2)}) %collective-permute-start.3) | collective-permute-done | bytes 32800 | tf_op jit(solution)/shard_map/ppermute | solution.py:253
  23.3 2.7 %collective-permute-start.6 = (bf16[64,256]{1,0:T(8,128)(2,1)S(1)}, bf16[64,256]{1,0:T(8,128)(2,1)S(1)}, u32[]{:S(2)}, u32[]{:S(2)}) collective-permute-start(bf16[64,256]{1,0:T(8,128)(2,1)S(1)} %add_convert_fusion.sum_ref), channel_id=1, source_target_pairs={{0,8},{1,9},{2,10},{3,11},{4,12},{5,13},{6,14},{7,15},{8,0},{9,1},... | collective-permute-start | bytes 98312 | tf_op jit(solution)/shard_map/ppermute | solution.py:253
  25.9 2.1 %codes_step.3 = (bf16[64,128,256]{2,1,0:T(8,128)(2,1)}, bf16[64,256]{1,0:T(8,128)(2,1)S(1)}) custom-call(bf16[64,256]{1,0:T(8,128)(2,1)S(1)} %add_convert_fusion.sum_ref, bf16[64,128,256]{2,1,0:T(8,128)(2,1)S(1)} %get-tuple-element.14.codes_ref, bf16[64,16,512]{2,1,0:T(8,128)(2,1)S(1)} %get-tuple-element.20.shifted_ref, ...), custom_call_target="tpu_custom_call", output_to_operand_aliasing={{0}: (4, {})} | custom-call | flops 469762048 | bytes 3670016 | tf_op jit(solution)/shard_map/codes_step/pallas_call | solution.py:199
  28.1 0.1 collective-permute-done.6.last_ref
  28.1 0.1 normalize.1.mine_ref
  28.3 0.1 collective-permute-start.7
  28.3 1.2 %collective-permute-done.7.other_ref = f32[64,256]{1,0:T(8,128)S(1)} collective-permute-done((f32[64,256]{1,0:T(8,128)S(1)}, f32[64,256]{1,0:T(8,128)S(1)}, u32[]{:S(2)}, u32[]{:S(2)}) %collective-permute-start.7) | collective-permute-done | bytes 65568 | tf_op jit(solution)/shard_map/ppermute | solution.py:253
  29.6 0.7 %join.1 = f32[128,256]{1,0:T(8,128)} custom-call(f32[64,256]{1,0:T(8,128)S(1)} %normalize.1.mine_ref, f32[64,256]{1,0:T(8,128)S(1)} %collective-permute-done.7.other_ref), custom_call_target="tpu_custom_call" | custom-call | tf_op jit(solution)/shard_map/join/pallas_call | solution.py:327
  (2 shorter events, 0.0 us)
Async XLA Ops:
  4.8 1.4 %collective-permute-start = (f32[64,256]{1,0:T(8,128)S(1)}, f32[64,256]{1,0:T(8,128)S(1)}, u32[]{:S(2)}, u32[]{:S(2)}) collective-permute-start(f32[64,256]{1,0:T(8,128)S(1)} %get-tuple-element.15.sent_near_ref), channel_id=1, source_target_pairs={{0,1},{1,0},{2,3},{3,2},{4,5},{5,4},{6,7},{7,6},{8,9},{9,8},{10,11... | collective-permute-start | bytes 196616 | tf_op jit(solution)/shard_map/ppermute | solution.py:253
  5.4 0.7 %collective-permute-start.1 = (bf16[64,256]{1,0:T(8,128)(2,1)S(1)}, bf16[64,256]{1,0:T(8,128)(2,1)S(1)}, u32[]{:S(2)}, u32[]{:S(2)}) collective-permute-start(bf16[64,256]{1,0:T(8,128)(2,1)S(1)} %get-tuple-element.17), channel_id=1, source_target_pairs={{1,2},{3,4},{5,6},{7,8},{9,10},{11,12},{13,14},{2,1},{4,3},{6,5},{... | collective-permute-start | bytes 98312 | tf_op jit(solution)/shard_map/ppermute | solution.py:288
  8.6 6.2 %collective-permute-start.2 = (f32[64,256]{1,0:T(8,128)S(1)}, f32[64,256]{1,0:T(8,128)S(1)}, u32[]{:S(2)}, u32[]{:S(2)}) collective-permute-start(f32[64,256]{1,0:T(8,128)S(1)} %get-tuple-element.19), channel_id=1, source_target_pairs={{0,1},{1,0},{2,3},{3,2},{4,5},{5,4},{6,7},{7,6},{8,9},{9,8},{10,11... | collective-permute-start | bytes 196616 | tf_op jit(solution)/shard_map/ppermute | solution.py:253
  14.8 7.2 %collective-permute-start.5 = (bf16[64,256]{1,0:T(8,128)(2,1)S(1)}, bf16[64,256]{1,0:T(8,128)(2,1)S(1)}, u32[]{:S(2)}, u32[]{:S(2)}) collective-permute-start(bf16[64,256]{1,0:T(8,128)(2,1)S(1)} %add_convert_fusion.1.sum_ref), channel_id=1, source_target_pairs={{0,6},{1,7},{2,4},{3,5},{4,2},{5,3},{6,0},{7,1},{8,14},{9,15},{10,... | collective-permute-start | bytes 98312 | tf_op jit(solution)/shard_map/ppermute | solution.py:253
  18.9 3.9 %collective-permute-start.4 = (bf16[64,256]{1,0:T(8,128)(2,1)S(1)}, bf16[64,256]{1,0:T(8,128)(2,1)S(1)}, u32[]{:S(2)}, u32[]{:S(2)}) collective-permute-start(bf16[64,256]{1,0:T(8,128)(2,1)S(1)} %add_convert_fusion.1.sum_ref), channel_id=1, source_target_pairs={{0,4},{1,5},{2,6},{3,7},{4,0},{5,1},{6,2},{7,3},{8,12},{9,13},{10,... | collective-permute-start | bytes 98312 | tf_op jit(solution)/shard_map/ppermute | solution.py:253
  19.3 3.9 %collective-permute-start.3 = (bf16[64,256]{1,0:T(8,128)(2,1)S(1)}, bf16[64,256]{1,0:T(8,128)(2,1)S(1)}, u32[]{:S(2)}, u32[]{:S(2)}) collective-permute-start(bf16[64,256]{1,0:T(8,128)(2,1)S(1)} %add_convert_fusion.1.sum_ref), channel_id=1, source_target_pairs={{0,2},{1,3},{2,0},{3,1},{4,6},{5,7},{6,4},{7,5},{8,10},{9,11},{10,... | collective-permute-start | bytes 98312 | tf_op jit(solution)/shard_map/ppermute | solution.py:253
  23.3 4.9 %collective-permute-start.6 = (bf16[64,256]{1,0:T(8,128)(2,1)S(1)}, bf16[64,256]{1,0:T(8,128)(2,1)S(1)}, u32[]{:S(2)}, u32[]{:S(2)}) collective-permute-start(bf16[64,256]{1,0:T(8,128)(2,1)S(1)} %add_convert_fusion.sum_ref), channel_id=1, source_target_pairs={{0,8},{1,9},{2,10},{3,11},{4,12},{5,13},{6,14},{7,15},{8,0},{9,1},... | collective-permute-start | bytes 98312 | tf_op jit(solution)/shard_map/ppermute | solution.py:253
  28.3 1.3 %collective-permute-start.7 = (f32[64,256]{1,0:T(8,128)S(1)}, f32[64,256]{1,0:T(8,128)S(1)}, u32[]{:S(2)}, u32[]{:S(2)}) collective-permute-start(f32[64,256]{1,0:T(8,128)S(1)} %normalize.1.mine_ref), channel_id=1, source_target_pairs={{0,1},{1,0},{2,3},{3,2},{4,5},{5,4},{6,7},{7,6},{8,9},{9,8},{10,11... | collective-permute-start | bytes 196616 | tf_op jit(solution)/shard_map/ppermute | solution.py:253
